TPU v7x, 32 devices: a whole 2x2x4 slice. The times are simulated.
32 devices in a mesh: comp: 2 (over x), gx: 8 (over z, core), gy: 2 (over y).
Axes of the slice: x: 2, y: 2, z: 4, core: 2. Of those that a mesh axis runs over, the one named last changes fastest.
Arguments:
- state: float32 [2, 2, 64, 128, 256], P('comp', None, None, 'gx', 'gy'), may hold values from -6 to 6
- diffusion: float32 [2, 128, 256], P('comp', 'gx', 'gy'), may hold values from 0.03 to 0.15
- vertical: float32 [2, 64], P('comp'), may hold values from 0.01 to 0.1
- coupling: float32 [2, 128, 256], P('comp', 'gx', 'gy'), may hold values from 0.02 to 0.2
- land_sea: int32 [2, 128, 256], P('comp', 'gx', 'gy'), may hold values 0 or 1
- route_tile: int32 [2, 16, 64, 1], P('comp', ('gx', 'gy')), may hold values from 0 to 15; in each aligned block of 64 rows (0 to 63, 64 to 127, ..., all dimensions but the last counted through in order) at most 8 rows name the same one
- route_src: int32 [2, 16, 64], P('comp', ('gx', 'gy')), may hold values from 0 to 15
- route_dst: int32 [2, 16, 64], P('comp', ('gx', 'gy')), may hold values from 0 to 15
- pair_cols: int32 [2, 16, 64], P('comp', ('gx', 'gy')), may hold values from 64 to 128
- intersection: bfloat16 [2, 16, 64, 128, 128], P('comp', ('gx', 'gy')), may hold values from 0 to 0.03125
Outputs:
- final_state: float32 [2, 2, 64, 128, 256], P('comp', None, None, 'gx', 'gy')
Inputs may be any that keep to these rules, and one draw needn't show every extreme that they name: `route_tile`: within the 64 pairs of one component's tile no destination tile is named more than 8 times.
All inputs are finite; a program needn't handle non-finite values. No bound on the sum of `land_sea` on one device may be relied on, other than what follows from the above.
Results may differ from a plain program's by a relative error of at most 0.0003.
Values sent between devices are 32-bit elements; how exact they have to be, the bound alone decides.
A program may use at most 128 MiB of HBM per device.

v0:
```python
import jax
import jax.numpy as jnp
from jax import lax
from jax.sharding import PartitionSpec as P

SUBSTEPS = 3
INTERVALS = 2


def passed_along(value, axis, steps):
    count = lax.axis_size(axis)
    pairs = [(source, (source + steps) % count) for source in range(count)]
    return lax.ppermute(value, axis, pairs)


def from_partner(value, axis, apart):
    mask = 2**apart
    pairs = [(source, source ^ mask) for source in range(lax.axis_size(axis))]
    return lax.ppermute(value, axis, pairs)


def padded_2(shard, sides, width):
    for axis, dim in sides:
        devices, length = (lax.axis_size(axis), shard.shape[dim])
        up = [(i, (i + 1) % devices) for i in range(devices)]
        down = [(j, i) for i, j in up]
        last = lax.slice_in_dim(shard, length - width, length, axis=dim)
        initial = lax.slice_in_dim(shard, 0, width, axis=dim)
        before = lax.ppermute(last, axis, up)
        after = lax.ppermute(initial, axis, down)
        shard = jnp.concatenate([before, shard, after], axis=dim)
    return shard


def advance(padded, diff_num, mix_num, couple_num, gate, target):
    below = passed_along(padded[:, :, :, -1:], "gy", 1)
    above = passed_along(padded[:, :, :, :1], "gy", -1)
    center = padded[:, :, 1:-1]
    levels = center.shape[1]
    width_y = center.shape[3]
    lanes = jnp.arange(width_y)[None, None, None, :]
    north = jnp.where(lanes == width_y - 1, above[:, :, 1:-1], jnp.roll(center, -1, axis=3))
    south = jnp.where(lanes == 0, below[:, :, 1:-1], jnp.roll(center, 1, axis=3))
    lap_h = padded[:, :, 2:] + padded[:, :, :-2] + north + south - 4.0 * center
    level_ids = jnp.arange(levels)[None, :, None, None]
    upper = jnp.where(level_ids == levels - 1, center, jnp.roll(center, -1, axis=1))
    lower = jnp.where(level_ids == 0, center, jnp.roll(center, 1, axis=1))
    lap_v = upper - 2.0 * center + lower
    tend = diff_num[None, None] * lap_h + mix_num[None, :, None, None] * lap_v
    force = couple_num[None] * (target - center[:, 0])
    tend = tend + jnp.where(level_ids == 0, force[:, None], 0.0)
    return center + gate[None, None] * tend


def densify(got_vals, got_labels, block_ids):
    onehot = (got_labels[:, None] == block_ids[None, :]).astype(jnp.float32)
    return jnp.einsum("rb,rkc->kbc", onehot, got_vals, precision=lax.Precision.HIGHEST)


def body(
    state,
    diffusion,
    vertical,
    coupling,
    land_sea,
    route_tile,
    route_src,
    route_dst,
    pair_cols,
    intersection,
):
    section = lax.axis_index("comp")
    fields = state[0]
    tracers, levels, width_x, width_y = fields.shape
    lon_tiles = lax.axis_size("gx")
    lat_tiles = lax.axis_size("gy")
    tiles = lon_tiles * lat_tiles
    pairs = route_src.shape[2]
    slots = max(2, 2 * pairs // tiles)
    blocks = width_x * width_y // 128
    diff_num = diffusion[0]
    couple_num = coupling[0]
    mix_num = vertical[0]
    sea = land_sea[0].astype(jnp.float32)
    gate = jnp.where(section == 1, sea, jnp.ones_like(sea))
    dests = route_tile[0, 0, :, 0]
    sources = route_src[0, 0]
    dest_blocks = route_dst[0, 0]
    live_cols = pair_cols[0, 0]
    weights = intersection[0, 0]
    pair_ids = jnp.arange(pairs)
    same_dest = (dests[:, None] == dests[None, :]) & (pair_ids[:, None] > pair_ids[None, :])
    rank = jnp.sum(same_dest.astype(jnp.int32), axis=1)
    place = dests * slots + rank
    rowmask = (jnp.arange(128)[None, :] < live_cols[:, None]).astype(jnp.float32)
    block_ids = jnp.arange(blocks).astype(jnp.float32)
    for interval in range(INTERVALS):
        surface = fields[:, 0].astype(jnp.bfloat16)
        picked = surface[:, sources]
        contrib = (
            jnp.einsum("pij,kpj->pki", weights, picked, preferred_element_type=jnp.float32)
            * rowmask[:, None, :]
        )
        send_vals = jnp.zeros((tiles * slots, tracers, 128), jnp.float32).at[place].set(contrib)
        send_labels = (
            jnp.full((tiles * slots,), -1.0, jnp.float32)
            .at[place]
            .set(dest_blocks.astype(jnp.float32))
        )
        phased = (
            lax.all_to_all(
                send_vals.reshape(tiles, slots, tracers, 128),
                ("gx", "gy"),
                split_axis=0,
                concat_axis=0,
                tiled=True,
            ),
            lax.all_to_all(
                send_labels.reshape(tiles, slots),
                ("gx", "gy"),
                split_axis=0,
                concat_axis=0,
                tiled=True,
            ),
        )
        dense = densify(
            phased[0].reshape(tiles * slots, tracers, 128),
            phased[1].reshape(tiles * slots),
            block_ids,
        )
        arrived = from_partner(dense, "comp", 0)
        target = sea[None] * arrived
        for sub in range(SUBSTEPS):
            padded = padded_2(fields, (("gx", 2),), 1)
            fields = advance(padded, diff_num, mix_num, couple_num, gate, target)
    return fields[None]


def solution(mesh):
    in_specs = (
        P("comp", None, None, "gx", "gy"),
        P("comp", "gx", "gy"),
        P("comp", None),
        P("comp", "gx", "gy"),
        P("comp", "gx", "gy"),
        P("comp", ("gx", "gy"), None, None),
        P("comp", ("gx", "gy"), None),
        P("comp", ("gx", "gy"), None),
        P("comp", ("gx", "gy"), None),
        P("comp", ("gx", "gy"), None, None, None),
    )
    out_specs = P("comp", None, None, "gx", "gy")
    return jax.shard_map(body, mesh=mesh, in_specs=in_specs, out_specs=out_specs, check_vma=False)
```

profile of v0, /device:TPU:0, one launch (start us, length us, event | category | flops | bytes accessed | tf_op | source)
XLA Modules:
  0.0 199.8 jit_solution(16542454336677371759)
XLA Ops:
  3.8 7.4 %all-to-all-start.1 = ((f32[16,1,8]{2,1,0:T(1,128)}), f32[16,1,8]{2,1,0:T(1,128)}, u32[]{:S(2)}, u32[]{:S(2)}) async-start(f32[16,1,8]{2,1,0:T(1,128)} %bitcast.21), calls=%async_computation.1 | async-start | bytes 16384 | tf_op jit(solution)/shard_map/all_to_all | solution.py:118
  13.4 3.4 %collective-permute-start = (f32[2,64,1,128]{3,2,0,1:T(1,128)}, f32[2,64,1,128]{3,2,0,1:T(1,128)S(1)}, u32[]{:S(2)}, u32[]{:S(2)}) collective-permute-start(f32[2,64,1,128]{3,2,0,1:T(1,128)} %get-tuple-element.75), channel_id=1, source_target_pairs={{2,0},{4,2},{6,4},{8,6},{10,8},{12,10},{14,12},{0,14},{3,1},{5,3},... | collective-permute-start | bytes 196616 | tf_op jit(solution)/shard_map/ppermute | solution.py:30
  18.5 1.7 fusion.143
  26.2 2.6 %scatter_fusion = f32[128,2,128]{2,1,0:T(2,128)S(1)} fusion(f32[128,2,128]{2,1,0:T(2,128)S(1)} %broadcast.122.clone, s32[64]{0:T(128)} %copy-done.18, f32[64,2,128]{2,1,0:T(2,128)S(1)} %fusion.4), kind=kCustom, calls=%fused_computation.2 | custom fusion | bytes 196864 | tf_op jit(solution)/shard_map/scatter | solution.py:104
  29.4 5.8 %all-to-all-start = ((f32[16,8,2,128]{3,1,2,0:T(8,128)}), f32[16,8,2,128]{3,1,2,0:T(8,128)S(1)}, u32[]{:S(2)}, u32[]{:S(2)}) async-start(f32[16,8,2,128]{3,1,2,0:T(8,128)} %copy.98), calls=%async_computation | async-start | bytes 262144 | tf_op jit(solution)/shard_map/all_to_all | solution.py:111
  37.4 2.2 %fusion.114 = (f32[2,64,18,1]{3,2,0,1:T(8,128)}, f32[2,64,18,1]{3,2,0,1:T(8,128)}) fusion(f32[2,64,18,128]{3,2,0,1:T(8,128)S(1)} %pad_maximum_fusion), kind=kLoop, calls=%fused_computation.195 | loop fusion | bytes 36864 | tf_op jit(solution)/shard_map/slice | solution.py:37
  39.6 1.9 copy.91
  41.5 2.0 collective-permute-start.2
  43.5 2.5 %copy.94 = f32[2,64,18,1]{1,0,3,2:T(2,128)} copy(f32[2,64,18,1]{3,2,0,1:T(8,128)} %get-tuple-element.16) | data formatting | bytes 18432 | tf_op jit(solution)/shard_map/slice | solution.py:36
  50.9 4.4 %fusion.64 = f32[2,64,16,128]{3,2,0,1:T(8,128)S(1)} fusion(f32[2,64,16,128]{3,2,0,1:T(8,128)S(1)} %bitcast.131, f32[2,64,1,128]{3,2,0,1:T(1,128)S(1)} %collective-permute-done.1, f32[2,64,1,128]{3,2,0,1:T(1,128)S(1)} %collective-permute-done, f32[2,64,16,1]{3,2,0,1:T(8,128)} %get-tuple-element.72, f32[2,64,16,127]{3,2,0,1:T(8,128)} %get-tuple-element.74, ...), kind=kLoop, calls=%fused_computation.84 | loop fusion | flops 6553600 | bytes 6472320 | tf_op jit(solution)/shard_map/add | solution.py:52
  60.5 2.4 %collective-permute-start.5 = (f32[2,64,1,128]{3,2,0,1:T(1,128)S(1)}, f32[2,64,1,128]{3,2,0,1:T(1,128)S(1)}, u32[]{:S(2)}, u32[]{:S(2)}) collective-permute-start(f32[2,64,1,128]{3,2,0,1:T(1,128)S(1)} %get-tuple-element.65), channel_id=1, source_target_pairs={{2,0},{4,2},{6,4},{8,6},{10,8},{12,10},{14,12},{0,14},{3,1},{5,3},... | collective-permute-start | bytes 196616 | tf_op jit(solution)/shard_map/ppermute | solution.py:30
  62.9 1.9 collective-permute-done.5
  64.8 3.6 %collective-permute-done.6 = f32[2,64,1,128]{3,2,0,1:T(1,128)S(1)} collective-permute-done((f32[2,64,1,128]{3,2,0,1:T(1,128)S(1)}, f32[2,64,1,128]{3,2,0,1:T(1,128)S(1)}, u32[]{:S(2)}, u32[]{:S(2)}) %collective-permute-start.6) | collective-permute-done | bytes 65568 | tf_op jit(solution)/shard_map/ppermute | solution.py:29
  68.6 2.1 %fusion.113 = (f32[2,64,18,1]{3,2,0,1:T(8,128)}, f32[2,64,18,1]{3,2,0,1:T(8,128)}) fusion(f32[2,64,18,128]{3,2,0,1:T(8,128)S(1)} %pad_maximum_fusion.1), kind=kLoop, calls=%fused_computation.194 | loop fusion | bytes 36864 | tf_op jit(solution)/shard_map/slice | solution.py:37
  70.8 1.9 copy.101
  74.2 1.9 copy.104
  77.5 2.3 %collective-permute-done.8 = f32[2,64,18,1]{1,0,3,2:T(2,128)S(1)} collective-permute-done((f32[2,64,18,1]{1,0,3,2:T(2,128)S(1)}, f32[2,64,18,1]{1,0,3,2:T(2,128)S(1)}, u32[]{:S(2)}, u32[]{:S(2)}) %collective-permute-start.8) | collective-permute-done | bytes 9248 | tf_op jit(solution)/shard_map/ppermute | solution.py:13
  80.0 5.0 %fusion.55 = f32[2,64,16,128]{3,2,0,1:T(8,128)S(1)} fusion(f32[2,64,16,128]{3,2,0,1:T(8,128)} %copy-done.3, f32[2,64,1,128]{3,2,0,1:T(1,128)S(1)} %collective-permute-done.6, f32[2,64,1,128]{3,2,0,1:T(1,128)S(1)} %collective-permute-done.5, f32[2,64,16,1]{3,2,0,1:T(8,128)} %get-tuple-element.62, f32[2,64,16,127]{3,2,0,1:T(8,128)} %get-tuple-element.64, ...), kind=kLoop, calls=%fused_computation.73 | loop fusion | flops 6553600 | bytes 6472320 | tf_op jit(solution)/shard_map/add | solution.py:52
  86.8 1.7 fusion.133
  90.1 3.5 %collective-permute-start.9 = (f32[2,64,1,128]{3,2,0,1:T(1,128)S(1)}, f32[2,64,1,128]{3,2,0,1:T(1,128)S(1)}, u32[]{:S(2)}, u32[]{:S(2)}) collective-permute-start(f32[2,64,1,128]{3,2,0,1:T(1,128)S(1)} %get-tuple-element.55), channel_id=1, source_target_pairs={{2,0},{4,2},{6,4},{8,6},{10,8},{12,10},{14,12},{0,14},{3,1},{5,3},... | collective-permute-start | bytes 196616 | tf_op jit(solution)/shard_map/ppermute | solution.py:30
  93.7 1.9 collective-permute-done.10
  95.9 2.1 %fusion.112 = (f32[2,64,18,1]{3,2,0,1:T(8,128)}, f32[2,64,18,1]{3,2,0,1:T(8,128)}) fusion(f32[2,64,18,128]{3,2,0,1:T(8,128)S(1)} %pad_maximum_fusion.2), kind=kLoop, calls=%fused_computation.193 | loop fusion | bytes 36864 | tf_op jit(solution)/shard_map/slice | solution.py:37
  98.0 1.9 copy.107
  100.5 1.9 copy.110
  104.0 2.3 %collective-permute-done.12 = f32[2,64,18,1]{1,0,3,2:T(2,128)} collective-permute-done((f32[2,64,18,1]{1,0,3,2:T(2,128)S(1)}, f32[2,64,18,1]{1,0,3,2:T(2,128)}, u32[]{:S(2)}, u32[]{:S(2)}) %collective-permute-start.12) | collective-permute-done | bytes 9248 | tf_op jit(solution)/shard_map/ppermute | solution.py:13
  107.1 4.9 %fusion.46 = f32[2,64,16,128]{3,2,0,1:T(8,128)S(1)} fusion(f32[2,64,16,128]{3,2,0,1:T(8,128)} %copy-done.2, f32[2,64,1,128]{3,2,0,1:T(1,128)S(1)} %collective-permute-done.10, f32[2,64,1,128]{3,2,0,1:T(1,128)S(1)} %collective-permute-done.9, f32[2,64,16,1]{3,2,0,1:T(8,128)} %get-tuple-element.52, f32[2,64,16,127]{3,2,0,1:T(8,128)} %get-tuple-element.54, ...), kind=kLoop, calls=%fused_computation.62 | loop fusion | flops 6553600 | bytes 6472320 | tf_op jit(solution)/shard_map/add | solution.py:52
  114.5 1.7 fusion.128
  117.9 2.1 %collective-permute-start.13 = (f32[2,64,1,128]{3,2,0,1:T(1,128)}, f32[2,64,1,128]{3,2,0,1:T(1,128)S(1)}, u32[]{:S(2)}, u32[]{:S(2)}) collective-permute-start(f32[2,64,1,128]{3,2,0,1:T(1,128)} %get-tuple-element.45), channel_id=1, source_target_pairs={{2,0},{4,2},{6,4},{8,6},{10,8},{12,10},{14,12},{0,14},{3,1},{5,3},... | collective-permute-start | bytes 196616 | tf_op jit(solution)/shard_map/ppermute | solution.py:30
  122.0 2.4 %scatter_fusion.1 = f32[128,2,128]{2,1,0:T(2,128)S(1)} fusion(f32[128,2,128]{2,1,0:T(2,128)S(1)} %broadcast.122, s32[64]{0:T(128)S(1)} %copy-done.19, f32[64,2,128]{2,1,0:T(2,128)S(1)} %fusion.7), kind=kCustom, calls=%fused_computation.4 | custom fusion | bytes 196864 | tf_op jit(solution)/shard_map/scatter | solution.py:104
  125.1 5.8 %all-to-all-start.2 = ((f32[16,8,2,128]{3,1,2,0:T(8,128)}), f32[16,8,2,128]{3,1,2,0:T(8,128)S(1)}, u32[]{:S(2)}, u32[]{:S(2)}) async-start(f32[16,8,2,128]{3,1,2,0:T(8,128)} %copy.120), calls=%async_computation.2 | async-start | bytes 262144 | tf_op jit(solution)/shard_map/all_to_all | solution.py:111
  131.2 2.1 %fusion.111 = (f32[2,64,18,1]{3,2,0,1:T(8,128)}, f32[2,64,18,1]{3,2,0,1:T(8,128)}) fusion(f32[2,64,18,128]{3,2,0,1:T(8,128)S(1)} %pad_maximum_fusion.3), kind=kLoop, calls=%fused_computation.192 | loop fusion | bytes 36864 | tf_op jit(solution)/shard_map/slice | solution.py:37
  133.4 2.0 %copy.113 = f32[2,64,18,1]{1,0,3,2:T(2,128)S(1)} copy(f32[2,64,18,1]{3,2,0,1:T(8,128)} %get-tuple-element.9) | data formatting | bytes 18432 | tf_op jit(solution)/shard_map/slice | solution.py:37
  135.4 2.0 collective-permute-start.15
  139.6 2.1 %collective-permute-done.16 = f32[2,64,18,1]{1,0,3,2:T(2,128)S(1)} collective-permute-done((f32[2,64,18,1]{1,0,3,2:T(2,128)S(1)}, f32[2,64,18,1]{1,0,3,2:T(2,128)S(1)}, u32[]{:S(2)}, u32[]{:S(2)}) %collective-permute-start.16) | collective-permute-done | bytes 9248 | tf_op jit(solution)/shard_map/ppermute | solution.py:13
  142.4 4.3 %fusion.37 = f32[2,64,16,128]{3,2,0,1:T(8,128)S(1)} fusion(f32[2,64,16,128]{3,2,0,1:T(8,128)S(1)} %fusion.46, f32[2,64,1,128]{3,2,0,1:T(1,128)S(1)} %collective-permute-done.14, f32[2,64,1,128]{3,2,0,1:T(1,128)S(1)} %collective-permute-done.13, f32[2,64,16,1]{3,2,0,1:T(8,128)} %get-tuple-element.42, f32[2,64,16,127]{3,2,0,1:T(8,128)} %get-tuple-element.44, ...), kind=kLoop, calls=%fused_computation.51 | loop fusion | flops 6553600 | bytes 6472320 | tf_op jit(solution)/shard_map/add | solution.py:52
  148.2 1.7 fusion.123
  152.9 2.1 %collective-permute-done.18 = f32[2,64,1,128]{3,2,0,1:T(1,128)S(1)} collective-permute-done((f32[2,64,1,128]{3,2,0,1:T(1,128)S(1)}, f32[2,64,1,128]{3,2,0,1:T(1,128)S(1)}, u32[]{:S(2)}, u32[]{:S(2)}) %collective-permute-start.18) | collective-permute-done | bytes 65568 | tf_op jit(solution)/shard_map/ppermute | solution.py:30
  155.0 3.4 %collective-permute-done.19 = f32[2,64,1,128]{3,2,0,1:T(1,128)S(1)} collective-permute-done((f32[2,64,1,128]{3,2,0,1:T(1,128)S(1)}, f32[2,64,1,128]{3,2,0,1:T(1,128)S(1)}, u32[]{:S(2)}, u32[]{:S(2)}) %collective-permute-start.19) | collective-permute-done | bytes 65568 | tf_op jit(solution)/shard_map/ppermute | solution.py:29
  158.6 2.1 %fusion.110 = (f32[2,64,18,1]{3,2,0,1:T(8,128)}, f32[2,64,18,1]{3,2,0,1:T(8,128)}) fusion(f32[2,64,18,128]{3,2,0,1:T(8,128)S(1)} %pad_maximum_fusion.4), kind=kLoop, calls=%fused_computation.191 | loop fusion | bytes 36864 | tf_op jit(solution)/shard_map/slice | solution.py:37
  160.8 1.9 copy.122
  164.2 1.9 copy.125
  166.8 3.1 %collective-permute-done.21 = f32[2,64,18,1]{1,0,3,2:T(2,128)S(1)} collective-permute-done((f32[2,64,18,1]{1,0,3,2:T(2,128)S(1)}, f32[2,64,18,1]{1,0,3,2:T(2,128)S(1)}, u32[]{:S(2)}, u32[]{:S(2)}) %collective-permute-start.21) | collective-permute-done | bytes 9248 | tf_op jit(solution)/shard_map/ppermute | solution.py:13
  170.0 4.1 %fusion.28 = f32[2,64,16,128]{3,2,0,1:T(8,128)S(1)} fusion(f32[2,64,16,128]{3,2,0,1:T(8,128)S(1)} %fusion.37, f32[2,64,1,128]{3,2,0,1:T(1,128)S(1)} %collective-permute-done.19, f32[2,64,1,128]{3,2,0,1:T(1,128)S(1)} %collective-permute-done.18, f32[2,64,16,1]{3,2,0,1:T(8,128)} %get-tuple-element.32, f32[2,64,16,127]{3,2,0,1:T(8,128)} %get-tuple-element.34, ...), kind=kLoop, calls=%fused_computation.40 | loop fusion | flops 6553600 | bytes 6472320 | tf_op jit(solution)/shard_map/add | solution.py:52
  179.8 1.8 collective-permute-done.22
  181.6 3.2 %collective-permute-done.23 = f32[2,64,1,128]{3,2,0,1:T(1,128)S(1)} collective-permute-done((f32[2,64,1,128]{3,2,0,1:T(1,128)S(1)}, f32[2,64,1,128]{3,2,0,1:T(1,128)S(1)}, u32[]{:S(2)}, u32[]{:S(2)}) %collective-permute-start.23) | collective-permute-done | bytes 65568 | tf_op jit(solution)/shard_map/ppermute | solution.py:29
  185.0 2.1 %fusion.109 = (f32[2,64,18,1]{3,2,0,1:T(8,128)}, f32[2,64,18,1]{3,2,0,1:T(8,128)}) fusion(f32[2,64,18,128]{3,2,0,1:T(8,128)S(1)} %pad_maximum_fusion.5), kind=kLoop, calls=%fused_computation.190 | loop fusion | bytes 36864 | tf_op jit(solution)/shard_map/slice | solution.py:37
  187.2 2.0 %copy.128 = f32[2,64,18,1]{1,0,3,2:T(2,128)S(1)} copy(f32[2,64,18,1]{3,2,0,1:T(8,128)} %get-tuple-element.5) | data formatting | bytes 18432 | tf_op jit(solution)/shard_map/slice | solution.py:37
  194.2 4.5 %fusion.19 = f32[1,2,64,16,128]{4,3,1,2,0:T(8,128)S(1)} fusion(f32[2,64,16,128]{3,2,0,1:T(8,128)S(1)} %fusion.28, f32[2,64,1,128]{3,2,0,1:T(1,128)S(1)} %collective-permute-done.23, f32[2,64,1,128]{3,2,0,1:T(1,128)S(1)} %collective-permute-done.22, f32[2,64,16,1]{3,2,0,1:T(8,128)} %get-tuple-element.22, f32[2,64,16,127]{3,2,0,1:T(8,128)} %get-tuple-element.24, ...), kind=kLoop, calls=%fused_computation.29 | loop fusion | flops 6553600 | bytes 6472320 | tf_op jit(solution)/shard_map/broadcast_in_dim | solution.py:136
  (194 shorter events, 65.3 us)
Async XLA Ops:
  0.0 24.4 %copy-start = (bf16[1,1,64,128,128]{4,3,2,1,0:T(8,128)(2,1)S(1)}, bf16[1,1,64,128,128]{4,3,2,1,0:T(8,128)(2,1)}, u32[]{:S(2)}) copy-start(bf16[1,1,64,128,128]{4,3,2,1,0:T(8,128)(2,1)} %param.19) | copy-start | bytes 6291460
  3.8 25.6 %all-to-all-start.1 = ((f32[16,1,8]{2,1,0:T(1,128)}), f32[16,1,8]{2,1,0:T(1,128)}, u32[]{:S(2)}, u32[]{:S(2)}) async-start(f32[16,1,8]{2,1,0:T(1,128)} %bitcast.21), calls=%async_computation.1 | async-start | bytes 16384 | tf_op jit(solution)/shard_map/all_to_all | solution.py:118
  13.4 23.7 %collective-permute-start = (f32[2,64,1,128]{3,2,0,1:T(1,128)}, f32[2,64,1,128]{3,2,0,1:T(1,128)S(1)}, u32[]{:S(2)}, u32[]{:S(2)}) collective-permute-start(f32[2,64,1,128]{3,2,0,1:T(1,128)} %get-tuple-element.75), channel_id=1, source_target_pairs={{2,0},{4,2},{6,4},{8,6},{10,8},{12,10},{14,12},{0,14},{3,1},{5,3},... | collective-permute-start | bytes 196616 | tf_op jit(solution)/shard_map/ppermute | solution.py:30
  16.8 20.3 %collective-permute-start.1 = (f32[2,64,1,128]{3,2,0,1:T(1,128)}, f32[2,64,1,128]{3,2,0,1:T(1,128)S(1)}, u32[]{:S(2)}, u32[]{:S(2)}) collective-permute-start(f32[2,64,1,128]{3,2,0,1:T(1,128)} %get-tuple-element.76), channel_id=1, source_target_pairs={{0,2},{2,4},{4,6},{6,8},{8,10},{10,12},{12,14},{14,0},{1,3},{3,5},... | collective-permute-start | bytes 196616 | tf_op jit(solution)/shard_map/ppermute | solution.py:29
  20.2 3.0 %copy-start.9 = (s32[1,16,128]{2,1,0:T(8,128)S(1)}, s32[1,16,128]{2,1,0:T(8,128)}, u32[]{:S(2)}) copy-start(s32[1,16,128]{2,1,0:T(8,128)} %param.14) | copy-start | bytes 24580
  29.4 16.7 %all-to-all-start = ((f32[16,8,2,128]{3,1,2,0:T(8,128)}), f32[16,8,2,128]{3,1,2,0:T(8,128)S(1)}, u32[]{:S(2)}, u32[]{:S(2)}) async-start(f32[16,8,2,128]{3,1,2,0:T(8,128)} %copy.98), calls=%async_computation | async-start | bytes 262144 | tf_op jit(solution)/shard_map/all_to_all | solution.py:111
  37.1 8.9 %copy-start.16 = (f32[128]{0:T(128)}, f32[128]{0:T(128)S(1)}, u32[]{:S(2)}) copy-start(f32[128]{0:T(128)S(1)} %eq.159) | copy-start | bytes 1540
  39.6 6.5 %copy-start.20 = (f32[16]{0:T(128)S(1)}, f32[16]{0:T(128)}, u32[]{:S(2)}) copy-start(f32[16]{0:T(128)} %iota_convert_fusion) | copy-start | bytes 196
  39.6 11.3 %copy-start.7 = (f32[1,16,128]{2,1,0:T(8,128)S(1)}, f32[1,16,128]{2,1,0:T(8,128)}, u32[]{:S(2)}) copy-start(f32[1,16,128]{2,1,0:T(8,128)} %param.13) | copy-start | bytes 24580
  39.6 11.3 %copy-start.6 = (f32[1,16,128]{2,1,0:T(8,128)S(1)}, f32[1,16,128]{2,1,0:T(8,128)}, u32[]{:S(2)}) copy-start(f32[1,16,128]{2,1,0:T(8,128)} %param.11) | copy-start | bytes 24580
  39.6 11.3 %copy-start.8 = (f32[2,1,16,128]{3,2,0,1:T(8,128)S(1)}, f32[2,1,16,128]{3,2,0,1:T(8,128)}, u32[]{:S(2)}) copy-start(f32[2,1,16,128]{3,2,0,1:T(8,128)} %get-tuple-element.68) | copy-start | bytes 49156
  41.5 7.4 %collective-permute-start.2 = (f32[2,64,18,1]{1,0,3,2:T(2,128)S(1)}, f32[2,64,18,1]{1,0,3,2:T(2,128)}, u32[]{:S(2)}, u32[]{:S(2)}) collective-permute-start(f32[2,64,18,1]{1,0,3,2:T(2,128)S(1)} %copy.91), channel_id=1, source_target_pairs={{0,1},{1,0},{2,3},{3,2},{4,5},{5,4},{6,7},{7,6},{8,9},{9,8},{10,11... | collective-permute-start | bytes 27656 | tf_op jit(solution)/shard_map/ppermute | solution.py:13
  46.0 4.1 %collective-permute-start.3 = (f32[2,64,18,1]{1,0,3,2:T(2,128)}, f32[2,64,18,1]{1,0,3,2:T(2,128)}, u32[]{:S(2)}, u32[]{:S(2)}) collective-permute-start(f32[2,64,18,1]{1,0,3,2:T(2,128)} %copy.94), channel_id=1, source_target_pairs={{0,1},{1,0},{2,3},{3,2},{4,5},{5,4},{6,7},{7,6},{8,9},{9,8},{10,11... | collective-permute-start | bytes 27656 | tf_op jit(solution)/shard_map/ppermute | solution.py:13
  46.9 4.0 %collective-permute-start.4 = (f32[2,16,128]{2,1,0:T(8,128)}, f32[2,16,128]{2,1,0:T(8,128)S(1)}, u32[]{:S(2)}, u32[]{:S(2)}) collective-permute-start(f32[2,16,128]{2,1,0:T(8,128)} %convolution_bitcast_fusion.1), channel_id=1, source_target_pairs={{0,16},{16,0},{1,17},{17,1},{2,18},{18,2},{3,19},{19,3},{4,20},{20... | collective-permute-start | bytes 49160 | tf_op jit(solution)/shard_map/ppermute | solution.py:19
  55.3 13.0 %copy-start.3 = (f32[2,64,16,128]{3,2,0,1:T(8,128)}, f32[2,64,16,128]{3,2,0,1:T(8,128)S(1)}, u32[]{:S(2)}) copy-start(f32[2,64,16,128]{3,2,0,1:T(8,128)S(1)} %fusion.64) | copy-start | bytes 3145732
  60.5 4.3 %collective-permute-start.5 = (f32[2,64,1,128]{3,2,0,1:T(1,128)S(1)}, f32[2,64,1,128]{3,2,0,1:T(1,128)S(1)}, u32[]{:S(2)}, u32[]{:S(2)}) collective-permute-start(f32[2,64,1,128]{3,2,0,1:T(1,128)S(1)} %get-tuple-element.65), channel_id=1, source_target_pairs={{2,0},{4,2},{6,4},{8,6},{10,8},{12,10},{14,12},{0,14},{3,1},{5,3},... | collective-permute-start | bytes 196616 | tf_op jit(solution)/shard_map/ppermute | solution.py:30
  62.8 5.5 %collective-permute-start.6 = (f32[2,64,1,128]{3,2,0,1:T(1,128)S(1)}, f32[2,64,1,128]{3,2,0,1:T(1,128)S(1)}, u32[]{:S(2)}, u32[]{:S(2)}) collective-permute-start(f32[2,64,1,128]{3,2,0,1:T(1,128)S(1)} %get-tuple-element.66), channel_id=1, source_target_pairs={{0,2},{2,4},{4,6},{6,8},{8,10},{10,12},{12,14},{14,0},{1,3},{3,5},... | collective-permute-start | bytes 196616 | tf_op jit(solution)/shard_map/ppermute | solution.py:29
  70.8 9.2 %copy-start.10 = (f32[1,64]{1,0:T(1,128)S(1)}, f32[1,64]{1,0:T(1,128)}, u32[]{:S(2)}) copy-start(f32[1,64]{1,0:T(1,128)} %param.12) | copy-start | bytes 772
  70.8 9.2 %copy-start.11 = (pred[64]{0:T(512)(128)(4,1)S(1)}, pred[64]{0:T(512)(128)(4,1)}, u32[]{:S(2)}) copy-start(pred[64]{0:T(512)(128)(4,1)} %get-tuple-element.77) | copy-start | bytes 196
  70.8 9.2 %copy-start.12 = (pred[64]{0:T(512)(128)(4,1)S(1)}, pred[64]{0:T(512)(128)(4,1)}, u32[]{:S(2)}) copy-start(pred[64]{0:T(512)(128)(4,1)} %get-tuple-element.78) | copy-start | bytes 196
  70.8 9.2 %copy-start.13 = (pred[128]{0:T(512)(128)(4,1)S(1)}, pred[128]{0:T(512)(128)(4,1)}, u32[]{:S(2)}) copy-start(pred[128]{0:T(512)(128)(4,1)} %get-tuple-element.79) | copy-start | bytes 388
  72.7 4.7 %collective-permute-start.7 = (f32[2,64,18,1]{1,0,3,2:T(2,128)S(1)}, f32[2,64,18,1]{1,0,3,2:T(2,128)S(1)}, u32[]{:S(2)}, u32[]{:S(2)}) collective-permute-start(f32[2,64,18,1]{1,0,3,2:T(2,128)S(1)} %copy.101), channel_id=1, source_target_pairs={{0,1},{1,0},{2,3},{3,2},{4,5},{5,4},{6,7},{7,6},{8,9},{9,8},{10,11... | collective-permute-start | bytes 27656 | tf_op jit(solution)/shard_map/ppermute | solution.py:13
  76.1 3.8 %collective-permute-start.8 = (f32[2,64,18,1]{1,0,3,2:T(2,128)S(1)}, f32[2,64,18,1]{1,0,3,2:T(2,128)S(1)}, u32[]{:S(2)}, u32[]{:S(2)}) collective-permute-start(f32[2,64,18,1]{1,0,3,2:T(2,128)S(1)} %copy.104), channel_id=1, source_target_pairs={{0,1},{1,0},{2,3},{3,2},{4,5},{5,4},{6,7},{7,6},{8,9},{9,8},{10,11... | collective-permute-start | bytes 27656 | tf_op jit(solution)/shard_map/ppermute | solution.py:13
  85.0 18.9 %copy-start.2 = (f32[2,64,16,128]{3,2,0,1:T(8,128)}, f32[2,64,16,128]{3,2,0,1:T(8,128)S(1)}, u32[]{:S(2)}) copy-start(f32[2,64,16,128]{3,2,0,1:T(8,128)S(1)} %fusion.55) | copy-start | bytes 3145732
  90.1 5.5 %collective-permute-start.10 = (f32[2,64,1,128]{3,2,0,1:T(1,128)S(1)}, f32[2,64,1,128]{3,2,0,1:T(1,128)S(1)}, u32[]{:S(2)}, u32[]{:S(2)}) collective-permute-start(f32[2,64,1,128]{3,2,0,1:T(1,128)S(1)} %get-tuple-element.56), channel_id=1, source_target_pairs={{0,2},{2,4},{4,6},{6,8},{8,10},{10,12},{12,14},{14,0},{1,3},{3,5},... | collective-permute-start | bytes 196616 | tf_op jit(solution)/shard_map/ppermute | solution.py:29
  90.1 5.5 %collective-permute-start.9 = (f32[2,64,1,128]{3,2,0,1:T(1,128)S(1)}, f32[2,64,1,128]{3,2,0,1:T(1,128)S(1)}, u32[]{:S(2)}, u32[]{:S(2)}) collective-permute-start(f32[2,64,1,128]{3,2,0,1:T(1,128)S(1)} %get-tuple-element.55), channel_id=1, source_target_pairs={{2,0},{4,2},{6,4},{8,6},{10,8},{12,10},{14,12},{0,14},{3,1},{5,3},... | collective-permute-start | bytes 196616 | tf_op jit(solution)/shard_map/ppermute | solution.py:30
  98.0 9.1 %copy-start.14 = (pred[128]{0:T(512)(128)(4,1)S(1)}, pred[128]{0:T(512)(128)(4,1)}, u32[]{:S(2)}) copy-start(pred[128]{0:T(512)(128)(4,1)} %get-tuple-element.80) | copy-start | bytes 388
  99.9 4.0 %collective-permute-start.11 = (f32[2,64,18,1]{1,0,3,2:T(2,128)S(1)}, f32[2,64,18,1]{1,0,3,2:T(2,128)S(1)}, u32[]{:S(2)}, u32[]{:S(2)}) collective-permute-start(f32[2,64,18,1]{1,0,3,2:T(2,128)S(1)} %copy.107), channel_id=1, source_target_pairs={{0,1},{1,0},{2,3},{3,2},{4,5},{5,4},{6,7},{7,6},{8,9},{9,8},{10,11... | collective-permute-start | bytes 27656 | tf_op jit(solution)/shard_map/ppermute | solution.py:13
  102.4 3.9 %collective-permute-start.12 = (f32[2,64,18,1]{1,0,3,2:T(2,128)S(1)}, f32[2,64,18,1]{1,0,3,2:T(2,128)}, u32[]{:S(2)}, u32[]{:S(2)}) collective-permute-start(f32[2,64,18,1]{1,0,3,2:T(2,128)S(1)} %copy.110), channel_id=1, source_target_pairs={{0,1},{1,0},{2,3},{3,2},{4,5},{5,4},{6,7},{7,6},{8,9},{9,8},{10,11... | collective-permute-start | bytes 27656 | tf_op jit(solution)/shard_map/ppermute | solution.py:13
  117.8 4.1 %copy-start.19 = (s32[64]{0:T(128)S(1)}, s32[64]{0:T(128)}, u32[]{:S(2)}) copy-start(s32[64]{0:T(128)} %copy-done.18) | copy-start | bytes 772
  117.9 13.1 %collective-permute-start.13 = (f32[2,64,1,128]{3,2,0,1:T(1,128)}, f32[2,64,1,128]{3,2,0,1:T(1,128)S(1)}, u32[]{:S(2)}, u32[]{:S(2)}) collective-permute-start(f32[2,64,1,128]{3,2,0,1:T(1,128)} %get-tuple-element.45), channel_id=1, source_target_pairs={{2,0},{4,2},{6,4},{8,6},{10,8},{12,10},{14,12},{0,14},{3,1},{5,3},... | collective-permute-start | bytes 196616 | tf_op jit(solution)/shard_map/ppermute | solution.py:30
  120.0 11.0 %collective-permute-start.14 = (f32[2,64,1,128]{3,2,0,1:T(1,128)S(1)}, f32[2,64,1,128]{3,2,0,1:T(1,128)S(1)}, u32[]{:S(2)}, u32[]{:S(2)}) collective-permute-start(f32[2,64,1,128]{3,2,0,1:T(1,128)S(1)} %get-tuple-element.46), channel_id=1, source_target_pairs={{0,2},{2,4},{4,6},{6,8},{8,10},{10,12},{12,14},{14,0},{1,3},{3,5},... | collective-permute-start | bytes 196616 | tf_op jit(solution)/shard_map/ppermute | solution.py:29
  125.1 13.3 %all-to-all-start.2 = ((f32[16,8,2,128]{3,1,2,0:T(8,128)}), f32[16,8,2,128]{3,1,2,0:T(8,128)S(1)}, u32[]{:S(2)}, u32[]{:S(2)}) async-start(f32[16,8,2,128]{3,1,2,0:T(8,128)} %copy.120), calls=%async_computation.2 | async-start | bytes 262144 | tf_op jit(solution)/shard_map/all_to_all | solution.py:111
  133.3 4.0 %copy-start.4 = (f32[2,64,18,1]{3,2,0,1:T(8,128)S(1)}, f32[2,64,18,1]{3,2,0,1:T(8,128)}, u32[]{:S(2)}) copy-start(f32[2,64,18,1]{3,2,0,1:T(8,128)} %get-tuple-element.10) | copy-start | bytes 27652
  133.3 5.1 %copy-start.17 = (f32[128]{0:T(128)S(1)}, f32[128]{0:T(128)}, u32[]{:S(2)}) copy-start(f32[128]{0:T(128)} %copy-done.16) | copy-start | bytes 1540
  133.4 5.1 %copy-start.21 = (f32[16]{0:T(128)S(1)}, f32[16]{0:T(128)}, u32[]{:S(2)}) copy-start(f32[16]{0:T(128)} %iota_convert_fusion) | copy-start | bytes 196
  135.4 4.1 %collective-permute-start.15 = (f32[2,64,18,1]{1,0,3,2:T(2,128)S(1)}, f32[2,64,18,1]{1,0,3,2:T(2,128)S(1)}, u32[]{:S(2)}, u32[]{:S(2)}) collective-permute-start(f32[2,64,18,1]{1,0,3,2:T(2,128)S(1)} %copy.113), channel_id=1, source_target_pairs={{0,1},{1,0},{2,3},{3,2},{4,5},{5,4},{6,7},{7,6},{8,9},{9,8},{10,11... | collective-permute-start | bytes 27656 | tf_op jit(solution)/shard_map/ppermute | solution.py:13
  137.9 3.8 %collective-permute-start.16 = (f32[2,64,18,1]{1,0,3,2:T(2,128)S(1)}, f32[2,64,18,1]{1,0,3,2:T(2,128)S(1)}, u32[]{:S(2)}, u32[]{:S(2)}) collective-permute-start(f32[2,64,18,1]{1,0,3,2:T(2,128)S(1)} %copy.116), channel_id=1, source_target_pairs={{0,1},{1,0},{2,3},{3,2},{4,5},{5,4},{6,7},{7,6},{8,9},{9,8},{10,11... | collective-permute-start | bytes 27656 | tf_op jit(solution)/shard_map/ppermute | solution.py:13
  138.6 3.8 %collective-permute-start.17 = (f32[2,16,128]{2,1,0:T(8,128)S(1)}, f32[2,16,128]{2,1,0:T(8,128)S(1)}, u32[]{:S(2)}, u32[]{:S(2)}) collective-permute-start(f32[2,16,128]{2,1,0:T(8,128)S(1)} %convolution_bitcast_fusion), channel_id=1, source_target_pairs={{0,16},{16,0},{1,17},{17,1},{2,18},{18,2},{3,19},{19,3},{4,20},{20... | collective-permute-start | bytes 49160 | tf_op jit(solution)/shard_map/ppermute | solution.py:19
  151.5 3.4 %collective-permute-start.18 = (f32[2,64,1,128]{3,2,0,1:T(1,128)S(1)}, f32[2,64,1,128]{3,2,0,1:T(1,128)S(1)}, u32[]{:S(2)}, u32[]{:S(2)}) collective-permute-start(f32[2,64,1,128]{3,2,0,1:T(1,128)S(1)} %get-tuple-element.35), channel_id=1, source_target_pairs={{2,0},{4,2},{6,4},{8,6},{10,8},{12,10},{14,12},{0,14},{3,1},{5,3},... | collective-permute-start | bytes 196616 | tf_op jit(solution)/shard_map/ppermute | solution.py:30
  152.9 5.5 %collective-permute-start.19 = (f32[2,64,1,128]{3,2,0,1:T(1,128)S(1)}, f32[2,64,1,128]{3,2,0,1:T(1,128)S(1)}, u32[]{:S(2)}, u32[]{:S(2)}) collective-permute-start(f32[2,64,1,128]{3,2,0,1:T(1,128)S(1)} %get-tuple-element.36), channel_id=1, source_target_pairs={{0,2},{2,4},{4,6},{6,8},{8,10},{10,12},{12,14},{14,0},{1,3},{3,5},... | collective-permute-start | bytes 196616 | tf_op jit(solution)/shard_map/ppermute | solution.py:29
  162.7 4.0 %collective-permute-start.20 = (f32[2,64,18,1]{1,0,3,2:T(2,128)S(1)}, f32[2,64,18,1]{1,0,3,2:T(2,128)S(1)}, u32[]{:S(2)}, u32[]{:S(2)}) collective-permute-start(f32[2,64,18,1]{1,0,3,2:T(2,128)S(1)} %copy.122), channel_id=1, source_target_pairs={{0,1},{1,0},{2,3},{3,2},{4,5},{5,4},{6,7},{7,6},{8,9},{9,8},{10,11... | collective-permute-start | bytes 27656 | tf_op jit(solution)/shard_map/ppermute | solution.py:13
  166.1 3.8 %collective-permute-start.21 = (f32[2,64,18,1]{1,0,3,2:T(2,128)S(1)}, f32[2,64,18,1]{1,0,3,2:T(2,128)S(1)}, u32[]{:S(2)}, u32[]{:S(2)}) collective-permute-start(f32[2,64,18,1]{1,0,3,2:T(2,128)S(1)} %copy.125), channel_id=1, source_target_pairs={{0,1},{1,0},{2,3},{3,2},{4,5},{5,4},{6,7},{7,6},{8,9},{9,8},{10,11... | collective-permute-start | bytes 27656 | tf_op jit(solution)/shard_map/ppermute | solution.py:13
  179.3 2.3 %collective-permute-start.22 = (f32[2,64,1,128]{3,2,0,1:T(1,128)S(1)}, f32[2,64,1,128]{3,2,0,1:T(1,128)S(1)}, u32[]{:S(2)}, u32[]{:S(2)}) collective-permute-start(f32[2,64,1,128]{3,2,0,1:T(1,128)S(1)} %get-tuple-element.25), channel_id=1, source_target_pairs={{2,0},{4,2},{6,4},{8,6},{10,8},{12,10},{14,12},{0,14},{3,1},{5,3},... | collective-permute-start | bytes 196616 | tf_op jit(solution)/shard_map/ppermute | solution.py:30
  179.3 5.5 %collective-permute-start.23 = (f32[2,64,1,128]{3,2,0,1:T(1,128)S(1)}, f32[2,64,1,128]{3,2,0,1:T(1,128)S(1)}, u32[]{:S(2)}, u32[]{:S(2)}) collective-permute-start(f32[2,64,1,128]{3,2,0,1:T(1,128)S(1)} %get-tuple-element.26), channel_id=1, source_target_pairs={{0,2},{2,4},{4,6},{6,8},{8,10},{10,12},{12,14},{14,0},{1,3},{3,5},... | collective-permute-start | bytes 196616 | tf_op jit(solution)/shard_map/ppermute | solution.py:29
  189.2 3.8 %collective-permute-start.24 = (f32[2,64,18,1]{1,0,3,2:T(2,128)S(1)}, f32[2,64,18,1]{1,0,3,2:T(2,128)S(1)}, u32[]{:S(2)}, u32[]{:S(2)}) collective-permute-start(f32[2,64,18,1]{1,0,3,2:T(2,128)S(1)} %copy.128), channel_id=1, source_target_pairs={{0,1},{1,0},{2,3},{3,2},{4,5},{5,4},{6,7},{7,6},{8,9},{9,8},{10,11... | collective-permute-start | bytes 27656 | tf_op jit(solution)/shard_map/ppermute | solution.py:13
  190.3 3.8 %collective-permute-start.25 = (f32[2,64,18,1]{1,0,3,2:T(2,128)S(1)}, f32[2,64,18,1]{1,0,3,2:T(2,128)S(1)}, u32[]{:S(2)}, u32[]{:S(2)}) collective-permute-start(f32[2,64,18,1]{1,0,3,2:T(2,128)S(1)} %copy.131), channel_id=1, source_target_pairs={{0,1},{1,0},{2,3},{3,2},{4,5},{5,4},{6,7},{7,6},{8,9},{9,8},{10,11... | collective-permute-start | bytes 27656 | tf_op jit(solution)/shard_map/ppermute | solution.py:13
  194.2 5.6 %copy-start.1 = (bf16[1,1,64,128,128]{4,3,2,1,0:T(8,128)(2,1)S(1)}, bf16[1,1,64,128,128]{4,3,2,1,0:T(8,128)(2,1)}, u32[]{:S(2)}) copy-start(bf16[1,1,64,128,128]{4,3,2,1,0:T(8,128)(2,1)} %param.19) | copy-start | bytes 6291460
  (5 other events, 11.1 us)
where the time goes:
time: 201 us; the launch traced here: 200 us
  local copies, waits for them, and re-layouts  83.1 us (41%)
  starting transfers between devices  47.3 us (24%)
  other arithmetic  34.3 us (17%)
  waiting for transfers between devices  31.1 us (15%)
  matrix products  3.34 us (2%)
    slice x12, local copies, waits for them, and re-layouts, advance(): above = passed_along(padded[:, :, :, :1], 'gy', -1)  24.6 us
    add x5, other arithmetic, advance(): return center + gate[None, None] * tend  22.8 us
    slice x12, local copies, waits for them, and re-layouts, advance(): jnp.roll(center, 1, axis=3)  20.1 us
    ppermute x6, starting transfers between devices, padded_2(): after = lax.ppermute(initial, axis, down)  12.8 us
    ppermute x12, starting transfers between devices, passed_along(): return lax.ppermute(value, axis, pairs)  12.6 us
    ppermute x12, waiting for transfers between devices, passed_along(): return lax.ppermute(value, axis, pairs)  12.3 us
    ppermute x6, waiting for transfers between devices, padded_2(): before = lax.ppermute(last, axis, up)  12.1 us
    all_to_all x2, starting transfers between devices, body(): lax.all_to_all(send_vals.reshape(tiles, slots, tracers, 128), ('gx', 'gy'...  11.6 us
  transfers between devices with their start and end apart: 29, of which 16 were waited for; matrix products, arithmetic and copies ran while one was open for 22% of the time, Pallas kernels for 0%

commit v1 on v0

v1 whole, which is shorter than its diff:
```python
import functools

import jax
import jax.numpy as jnp
from jax import lax
from jax.experimental import pallas as pl
from jax.experimental.pallas import tpu as pltpu
from jax.sharding import PartitionSpec as P

SUBSTEPS = 3
INTERVALS = 2
MESH = pl.DeviceIdType.MESH
HIGHEST = lax.Precision.HIGHEST
TOP = 8
SLAB = 8
LANES = 128
CHUNK = 4


def split_rows(value):
    first = value.astype(jnp.bfloat16)
    rest = value - first.astype(jnp.float32)
    second = rest.astype(jnp.bfloat16)
    third = (rest - second.astype(jnp.float32)).astype(jnp.bfloat16)
    return first, second, third


def pick(onehot, value):
    total = None
    for part in split_rows(value):
        term = jnp.dot(onehot, part, preferred_element_type=jnp.float32)
        total = term if total is None else total + term
    return total


def kernel(
    dims,
    state_ref,
    diff_ref,
    mix_ref,
    couple_ref,
    sea_ref,
    tile_ref,
    src_ref,
    dst_ref,
    cols_ref,
    weight_ref,
    out_ref,
    state_v,
    weight_v,
    *rest,
):
    n_gx, n_gy, tiles, rows, pairs, tracers, levels, width = dims
    count = INTERVALS * SUBSTEPS
    fields = rest[:count]
    rest = rest[count:]
    slabs = rest[: INTERVALS * (SUBSTEPS - 1)]
    rest = rest[INTERVALS * (SUBSTEPS - 1) :]
    pack_out = rest[:count]
    pack_in = rest[count : 2 * count]
    rest = rest[2 * count :]
    slab_count = INTERVALS * (SUBSTEPS - 1) + 1
    slab_out = rest[:slab_count]
    slab_in = rest[slab_count : 2 * slab_count]
    rest = rest[2 * slab_count :]
    sends = rest[:INTERVALS]
    recvs = rest[INTERVALS : 2 * INTERVALS]
    rest = rest[2 * INTERVALS :]
    (
        label_out,
        label_in,
        surf,
        contrib,
        gate_diff,
        gate_couple,
        gate_ref,
        mix_v,
        goal,
        onehot_v,
        dense_v,
        load_sem,
        halo_send,
        halo_recv,
        route_send,
        route_recv,
    ) = rest

    comp = lax.axis_index("comp")
    gx = lax.axis_index("gx")
    gy = lax.axis_index("gy")
    other = 1 - comp
    mine = gx * n_gy + gy
    right = (comp, lax.rem(gx + 1, n_gx), gy)
    left = (comp, lax.rem(gx + n_gx - 1, n_gx), gy)
    across = (comp, gx, lax.rem(gy + 1, n_gy))

    state_copy = pltpu.make_async_copy(state_ref, state_v, load_sem.at[0])
    state_copy.start()
    weight_copy = pltpu.make_async_copy(weight_ref, weight_v, load_sem.at[1])
    weight_copy.start()

    def peer(step):
        tile = lax.rem(mine + step, tiles)
        return tile, (other, tile // n_gy, lax.rem(tile, n_gy))

    barrier = pltpu.get_barrier_semaphore()
    for device in (right, left, across):
        pl.semaphore_signal(barrier, inc=1, device_id=device, device_id_type=MESH)

    def greet(step, carry):
        pl.semaphore_signal(barrier, inc=1, device_id=peer(step)[1], device_id_type=MESH)
        return carry

    lax.fori_loop(0, tiles, greet, 0)

    dest_col = jnp.broadcast_to(tile_ref[0, 0], (pairs, pairs))
    sub_ids = lax.broadcasted_iota(jnp.int32, (pairs, pairs), 0)
    lane_ids = lax.broadcasted_iota(jnp.int32, (pairs, pairs), 1)
    dest_row = jnp.sum(
        jnp.where(sub_ids == lane_ids, dest_col, 0).astype(jnp.float32), axis=0, keepdims=True
    )
    earlier = (dest_col.astype(jnp.float32) == dest_row) & (sub_ids < lane_ids)
    rank = jnp.sum(jnp.where(earlier, 1.0, 0.0), axis=0, keepdims=True)
    place = (dest_row * rows + rank).astype(jnp.int32)
    slot_ids = lax.broadcasted_iota(jnp.int32, (tiles * rows, pairs), 0)
    taken = slot_ids == place
    onehot_v[...] = jnp.where(taken, 1.0, 0.0).astype(jnp.bfloat16)
    labels = jnp.sum(
        jnp.where(taken, (dst_ref[0] + 1).astype(jnp.float32), 0.0), axis=1, keepdims=True
    )
    label_out[...] = jnp.broadcast_to(labels, (tiles * rows, LANES)).reshape(tiles, rows, LANES)

    sea = sea_ref[0].astype(jnp.float32)
    gate = jnp.where(comp == 1, sea, jnp.ones_like(sea))
    gate_ref[...] = gate
    gate_diff[...] = gate * diff_ref[0]
    gate_couple[...] = gate * couple_ref[0]
    level_a = lax.broadcasted_iota(jnp.int32, (levels, levels), 0)
    level_b = lax.broadcasted_iota(jnp.int32, (levels, levels), 1)
    mix_col = jnp.sum(
        jnp.where(level_a == level_b, jnp.broadcast_to(mix_ref[...], (levels, levels)), 0.0),
        axis=1,
        keepdims=True,
    )
    mix_v[...] = jnp.broadcast_to(mix_col, (levels, LANES))
    surf[...] = jnp.zeros(surf.shape, jnp.float32)

    def lane_of(height):
        return lax.broadcasted_iota(jnp.int32, (height, LANES), 1)

    def packed_lane(acc, value, place_j, height):
        turned = pltpu.roll(value, 2 * place_j + 1, 1)
        return jnp.where(lane_of(height) // 2 == place_j, turned, acc)

    def over_columns(body, acc):
        def step(chunk, acc):
            for i in range(CHUNK):
                for f in range(tracers):
                    acc = body(f, chunk * CHUNK + i, acc)
            return acc

        return lax.fori_loop(0, width // CHUNK, step, acc)

    def exchange(number, to_right, to_left, packs):
        copies = []
        for i, (src, dst, device) in enumerate(
            ((to_right[0], to_right[1], right), (to_left[0], to_left[1], left), (packs[0], packs[1], across))
        ):
            copy = pltpu.make_async_remote_copy(
                src_ref=src,
                dst_ref=dst,
                send_sem=halo_send.at[number, i],
                recv_sem=halo_recv.at[number, i],
                device_id=device,
                device_id_type=MESH,
            )
            copy.start()
            copies.append(copy)
        return copies

    def x_sides(buf, low, high):
        span = pl.ds(low, high - low)
        to_right = (buf.at[:, width, span, :], buf.at[:, 0, span, :])
        to_left = (buf.at[:, 1, span, :], buf.at[:, width + 1, span, :])
        return to_right, to_left

    started = []
    numbers = iter(range(64))

    def send_halo(buf, low, high, out, into):
        copies = exchange(next(numbers), *x_sides(buf, low, high), (out, into))
        started.extend(copies)
        return copies

    def stencil(buf, f, x, low, height, halo):
        center = buf[f, x + 1, low : low + height]
        after = buf[f, x + 2, low : low + height]
        before = buf[f, x, low : low + height]
        above = buf[f, x + 1, low - 1 : low - 1 + height]
        below = buf[f, x + 1, low + 1 : low + 1 + height]
        j = f * width + x
        turned = pltpu.roll(halo, LANES - 1 - 2 * j, 1)
        lanes = lane_of(height)
        north = pltpu.roll(jnp.where(lanes == 0, turned, center), LANES - 1, 1)
        south = pltpu.roll(jnp.where(lanes == LANES - 1, turned, center), 1, 1)
        lap_h = (after + before) + (north + south) - 4.0 * center
        lap_v = (below + above) - 2.0 * center
        row = pl.ds(x, 1)
        gd = jnp.broadcast_to(gate_diff[row, :], (height, LANES))
        gv = jnp.broadcast_to(gate_ref[row, :], (height, LANES)) * mix_v[low - TOP : low - TOP + height]
        return center, center + (gd * lap_h + gv * lap_v)

    def with_ends(buf, f, x, value, height):
        buf[f, x + 1, TOP - 1 : TOP] = value[0:1]
        buf[f, x + 1, TOP + height : TOP + height + 1] = value[height - 1 : height]

    pl.semaphore_wait(barrier, tiles + 3)

    def send_labels(step, carry):
        tile, device = peer(step)
        pltpu.make_async_remote_copy(
            src_ref=label_out.at[tile],
            dst_ref=label_in.at[mine],
            send_sem=route_send.at[INTERVALS],
            recv_sem=route_recv.at[INTERVALS],
            device_id=device,
            device_id_type=MESH,
        ).start()
        return carry

    lax.fori_loop(0, tiles, send_labels, 0)

    state_copy.wait()

    def load(f, x, acc):
        value = state_v[pl.ds(f * levels * width + x, levels, stride=width), :]
        fields[0][f, x + 1, TOP : TOP + levels] = value
        with_ends(fields[0], f, x, value, levels)
        surf[x, f : f + 1] = value[0:1]
        return packed_lane(acc, value, f * width + x, levels)

    pack_out[0][...] = over_columns(load, jnp.zeros((levels, LANES), jnp.float32))
    whole = (TOP, TOP + levels)
    pending = send_halo(fields[0], *whole, pack_out[0], pack_in[0])
    weight_copy.wait()

    def remap(interval):
        lanes = lane_of(SLAB)

        def one(group, carry):
            for i in range(8):
                p = group * 8 + i
                left_side = surf[src_ref[0, 0, p]].astype(jnp.bfloat16)
                got = lax.dot_general(
                    left_side,
                    weight_v[p],
                    (((1,), (1,)), ((), ())),
                    preferred_element_type=jnp.float32,
                )
                got = jnp.where(lanes < cols_ref[0, 0, p], got, 0.0)
                contrib[pl.ds(pl.multiple_of(p * 8, 8), 8), :] = got
            return carry

        lax.fori_loop(0, pairs // 8, one, 0)
        onehot = onehot_v[...]
        for f in range(tracers):
            value = contrib[pl.ds(f, pairs, stride=8), :]
            sends[interval][:, :, f * LANES : (f + 1) * LANES] = pick(onehot, value).reshape(
                tiles, rows, LANES
            )

        def post(step, carry):
            tile, device = peer(step)
            pltpu.make_async_remote_copy(
                src_ref=sends[interval].at[tile],
                dst_ref=recvs[interval].at[mine],
                send_sem=route_send.at[interval],
                recv_sem=route_recv.at[interval],
                device_id=device,
                device_id_type=MESH,
            ).start()
            return carry

        lax.fori_loop(0, tiles, post, 0)

    def wait_whole(ref, sem):
        pltpu.make_async_copy(ref, ref, sem).wait()

    zeros = jnp.zeros((levels, LANES), jnp.float32)
    slab_zeros = jnp.zeros((SLAB, LANES), jnp.float32)
    slab_number = 0
    slab_pending = []
    for interval in range(INTERVALS):
        final = interval == INTERVALS - 1
        remap(interval)
        first = interval * SUBSTEPS
        for sub in range(SUBSTEPS):
            for copy in pending:
                copy.wait_recv()
            pending = []
            if sub == 0:
                for copy in slab_pending:
                    copy.wait_recv()
                entry_slab = slab_in[slab_number - 1] if interval > 0 else None
                slab_pending = []
            buf = fields[first + sub]
            pack = pack_in[first + sub]
            if sub == 0 and interval > 0:
                pack[0:SLAB, :] = entry_slab[...]
            last = sub == SUBSTEPS - 1
            low = TOP + (SLAB if last else 0)
            height = levels - (SLAB if last else 0)
            halo_low = low - TOP

            def bulk(f, x, acc):
                _, value = stencil(buf, f, x, low, height, pack[halo_low:levels, :])
                if last and final:
                    start = f * levels * width + SLAB * width + x
                    out_ref[pl.ds(start, height, stride=width), :] = value
                    return acc
                after = fields[first + sub + 1]
                after[f, x + 1, low : low + height] = value
                if last:
                    after[f, x + 1, TOP + levels : TOP + levels + 1] = value[height - 1 : height]
                else:
                    with_ends(after, f, x, value, height)
                return packed_lane(acc, value, f * width + x, height)

            if last and final:
                over_columns(bulk, 0)
            else:
                packed = over_columns(bulk, zeros[0:height])
                pack_out[first + sub + 1][halo_low:levels, :] = packed
                part = (pack_out[first + sub + 1], pack_in[first + sub + 1])
                if last:
                    part = [ref.at[pl.ds(SLAB, height), :] for ref in part]
                pending = send_halo(fields[first + sub + 1], low, low + height, *part)

        if interval == 0:
            wait_whole(label_in, route_recv.at[INTERVALS])
            got_labels = label_in[...].reshape(tiles * rows, LANES)
            block_ids = lax.broadcasted_iota(jnp.int32, (tiles * rows, LANES), 1) + 1
            named = jnp.where(got_labels == block_ids.astype(jnp.float32), 1.0, 0.0)
            dense_v[...] = jnp.transpose(named)[0:width, :].astype(jnp.bfloat16)
        wait_whole(recvs[interval], route_recv.at[interval])
        dense = dense_v[...]
        for f in range(tracers):
            value = recvs[interval][:, :, f * LANES : (f + 1) * LANES].reshape(tiles * rows, LANES)
            goal[f] = sea * pick(dense, value)

        for sub in range(SUBSTEPS):
            for copy in slab_pending:
                copy.wait_recv()
            slab_pending = []
            index = interval * (SUBSTEPS - 1) + sub - 1
            if sub == 0:
                buf = fields[first]
                halo_ref = pack_in[first]
            else:
                buf = slabs[index]
                halo_ref = slab_in[slab_number - 1]
            last = sub == SUBSTEPS - 1

            def near(f, x, acc):
                center, value = stencil(buf, f, x, TOP, SLAB, halo_ref[0:SLAB, :])
                row = pl.ds(x, 1)
                force = jnp.broadcast_to(gate_couple[row, :], (SLAB, LANES)) * (
                    jnp.broadcast_to(goal[f, row, :], (SLAB, LANES)) - center
                )
                sub_row = lax.broadcasted_iota(jnp.int32, (SLAB, LANES), 0)
                value = value + jnp.where(sub_row == 0, force, 0.0)
                if last and final:
                    out_ref[pl.ds(f * levels * width + x, SLAB, stride=width), :] = value
                    return acc
                if last:
                    after = fields[first + SUBSTEPS]
                    surf[x, f : f + 1] = value[0:1]
                else:
                    after = slabs[index + 1]
                    after[f, x + 1, TOP + SLAB : TOP + SLAB + 1] = fields[first + sub + 1][
                        f, x + 1, TOP + SLAB : TOP + SLAB + 1
                    ]
                after[f, x + 1, TOP : TOP + SLAB] = value
                after[f, x + 1, TOP - 1 : TOP] = value[0:1]
                return packed_lane(acc, value, f * width + x, SLAB)

            if last and final:
                over_columns(near, 0)
            else:
                slab_out[slab_number][...] = over_columns(near, slab_zeros)
                after = fields[first + SUBSTEPS] if last else slabs[index + 1]
                slab_pending = send_halo(
                    after, TOP, TOP + SLAB, slab_out[slab_number], slab_in[slab_number]
                )
                slab_number += 1

    for copy in started:
        copy.wait_send()
    for interval in range(INTERVALS):
        wait_whole(sends[interval], route_send.at[interval])
    wait_whole(label_out, route_send.at[INTERVALS])


def body(
    n_gx,
    n_gy,
    state,
    diffusion,
    vertical,
    coupling,
    land_sea,
    route_tile,
    route_src,
    route_dst,
    pair_cols,
    intersection,
):
    _, tracers, levels, width, lanes = state.shape
    assert lanes == LANES and n_gy == 2 and 2 * tracers * width <= LANES
    tiles = n_gx * n_gy
    pairs = route_src.shape[2]
    slots = max(2, 2 * pairs // tiles)
    rows = -(-slots // 8) * 8
    dims = (n_gx, n_gy, tiles, rows, pairs, tracers, levels, width)
    count = INTERVALS * SUBSTEPS
    slab_count = INTERVALS * (SUBSTEPS - 1) + 1
    f32 = jnp.float32
    scratch = [
        pltpu.VMEM((tracers * levels * width, LANES), f32),
        pltpu.VMEM(intersection.shape[2:], jnp.bfloat16),
    ]
    scratch += [pltpu.VMEM((tracers, width + 2, TOP + levels + 8, LANES), f32)] * count
    scratch += [pltpu.VMEM((tracers, width + 2, TOP + SLAB + 8, LANES), f32)] * (
        INTERVALS * (SUBSTEPS - 1)
    )
    scratch += [pltpu.VMEM((levels, LANES), f32)] * (2 * count)
    scratch += [pltpu.VMEM((SLAB, LANES), f32)] * (2 * slab_count)
    scratch += [pltpu.VMEM((tiles, rows, tracers * LANES), f32)] * (2 * INTERVALS)
    scratch += [
        pltpu.VMEM((tiles, rows, LANES), f32),
        pltpu.VMEM((tiles, rows, LANES), f32),
        pltpu.VMEM((width, 8, LANES), f32),
        pltpu.VMEM((pairs * 8, LANES), f32),
        pltpu.VMEM((width, LANES), f32),
        pltpu.VMEM((width, LANES), f32),
        pltpu.VMEM((width, LANES), f32),
        pltpu.VMEM((levels, LANES), f32),
        pltpu.VMEM((tracers, width, LANES), f32),
        pltpu.VMEM((tiles * rows, pairs), jnp.bfloat16),
        pltpu.VMEM((width, tiles * rows), jnp.bfloat16),
        pltpu.SemaphoreType.DMA((2,)),
        pltpu.SemaphoreType.DMA((count + slab_count, 3)),
        pltpu.SemaphoreType.DMA((count + slab_count, 3)),
        pltpu.SemaphoreType.DMA((INTERVALS + 1,)),
        pltpu.SemaphoreType.DMA((INTERVALS + 1,)),
    ]
    vmem = pl.BlockSpec(memory_space=pltpu.VMEM)
    smem = pl.BlockSpec(memory_space=pltpu.SMEM)
    hbm = pl.BlockSpec(memory_space=pl.ANY)
    out = pl.pallas_call(
        functools.partial(kernel, dims),
        out_shape=jax.ShapeDtypeStruct((tracers * levels * width, LANES), f32),
        in_specs=[hbm, vmem, vmem, vmem, vmem, vmem, smem, vmem, smem, hbm],
        out_specs=vmem,
        scratch_shapes=scratch,
        compiler_params=pltpu.CompilerParams(
            collective_id=0, has_side_effects=True, vmem_limit_bytes=48 * 2**20
        ),
        cost_estimate=pl.CostEstimate(flops=60_000_000, bytes_accessed=5_000_000, transcendentals=0),
        name="coupled_columns",
    )(
        state.reshape(tracers * levels * width, LANES),
        diffusion,
        vertical,
        coupling,
        land_sea,
        route_tile,
        route_src,
        route_dst,
        pair_cols,
        intersection.reshape(intersection.shape[2:]),
    )
    return out.reshape(state.shape)


def solution(mesh):
    in_specs = (
        P("comp", None, None, "gx", "gy"),
        P("comp", "gx", "gy"),
        P("comp", None),
        P("comp", "gx", "gy"),
        P("comp", "gx", "gy"),
        P("comp", ("gx", "gy"), None, None),
        P("comp", ("gx", "gy"), None),
        P("comp", ("gx", "gy"), None),
        P("comp", ("gx", "gy"), None),
        P("comp", ("gx", "gy"), None, None, None),
    )
    out_specs = P("comp", None, None, "gx", "gy")
    run = functools.partial(body, mesh.shape["gx"], mesh.shape["gy"])
    return jax.shard_map(run, mesh=mesh, in_specs=in_specs, out_specs=out_specs, check_vma=False)
```

time: 201 us -> 73.3 us (0.36)
  local copies, waits for them, and re-layouts: 83.1 us -> 9.24 us
  Pallas kernels: 0 us -> 63.7 us
  starting transfers between devices: 47.3 us -> 0 us
  other arithmetic: 34.3 us -> 0 us
  waiting for transfers between devices: 31.1 us -> 0 us
  matrix products: 3.34 us -> 0 us
    slice x60 -> x0, local copies, waits for them, and re-layouts: 69.1 us -> none  [the longest x12 24.6 us: advance(): above = passed_along(padded[:, :, :, :1], 'gy', -1)]
    pallas_call x0 -> x1, Pallas kernels: none -> 63.7 us  [body(): pl.pallas_call(functools.partial(kernel, dims), out_shape=jax.ShapeDtypeS...]
    ppermute x26 -> x0, waiting for transfers between devices: 30.7 us -> none  [the longest x12 12.3 us: passed_along(): return lax.ppermute(value, axis, pairs)]
    ppermute x26 -> x0, starting transfers between devices: 28.2 us -> none  [the longest x6 12.8 us: padded_2(): after = lax.ppermute(initial, axis, down)]
    add x5 -> x0, other arithmetic: 22.8 us -> none  [advance(): return center + gate[None, None] * tend]
    all_to_all x3 -> x0, starting transfers between devices: 19.1 us -> none  [the longest x2 11.6 us: body(): lax.all_to_all(send_vals.reshape(tiles, slots, tracers, 128), ('gx', 'gy'...]
    unnamed x61 -> x20, local copies, waits for them, and re-layouts: 1.98 us -> 9.24 us
    scatter x3 -> x0, local copies, waits for them, and re-layouts: 5.76 us -> none  [the longest x2 4.99 us: body(): jnp.zeros((tiles * slots, tracers, 128), jnp.float32).at[place].set(contrib)]
  transfers between devices with their start and end apart: 29 -> 0, of which waited for: 16 -> 0; matrix products, arithmetic and copies ran while one was open for 22% -> 0% of each run, Pallas kernels for 0% -> 0%
where the time goes in v1:
time: 73.3 us; the launch traced here: 72.9 us
  Pallas kernels  63.7 us (87%)
  local copies, waits for them, and re-layouts  9.24 us (13%)
    pallas_call x1, Pallas kernels, body(): pl.pallas_call(functools.partial(kernel, dims), out_shape=jax.ShapeDtypeS...  63.7 us
    unnamed x20, local copies, waits for them, and re-layouts  9.24 us

profile of v1, /device:TPU:0, one launch (start us, length us, event | category | flops | bytes accessed | tf_op | source)
XLA Modules:
  0.0 72.9 jit_solution(17887766482555955194)
XLA Ops:
  0.0 0.7 %copy.11.tile_ref = s32[1,1,64,1]{3,2,1,0:T(8,128)S(1)} copy(s32[1,1,64,1]{2,3,1,0:T(1,128)} %param.15) | data formatting | bytes 512 | tf_op args[5]
  0.7 0.0 copy-start
  0.7 1.6 %copy-done = bf16[1,1,64,128,128]{4,3,2,1,0:T(8,128)(2,1)S(1)} copy-done((bf16[1,1,64,128,128]{4,3,2,1,0:T(8,128)(2,1)S(1)}, bf16[1,1,64,128,128]{4,3,2,1,0:T(8,128)(2,1)}, u32[]{:S(2)}) %copy-start) | copy-done | bytes 2097176
  2.3 0.0 copy-start.1
  2.3 1.2 %copy-done.1 = f32[1,2,64,16,128]{4,3,2,1,0:T(8,128)S(1)} copy-done((f32[1,2,64,16,128]{4,3,2,1,0:T(8,128)S(1)}, f32[1,2,64,16,128]{4,3,2,1,0:T(8,128)}, u32[]{:S(2)}) %copy-start.1) | copy-done | bytes 1048600
  3.6 0.0 copy-start.2
  3.6 0.7 copy-done.2
  4.3 0.0 copy-start.3
  4.3 0.7 copy-done.3
  5.0 0.0 copy-start.4
  5.0 0.7 copy-done.4
  5.7 0.0 copy-start.5
  5.7 0.7 copy-done.5
  6.3 0.0 copy-start.6
  6.3 0.7 copy-done.6
  7.0 0.0 copy-start.7
  7.0 0.7 copy-done.7
  7.6 0.0 copy-start.8
  7.6 0.7 copy-done.8
  8.3 63.7 %coupled_columns.1 = f32[2048,128]{1,0:T(8,128)S(1)} custom-call(f32[2048,128]{1,0:T(8,128)S(1)} %bitcast.5, f32[1,16,128]{2,1,0:T(8,128)S(1)} %copy-done.2, f32[1,64]{1,0:T(1,128)S(1)} %copy-done.5, f32[1,16,128]{2,1,0:T(8,128)S(1)} %copy-done.3, s32[1,16,128]{2,1,0:T(8,128)S(1)} %copy-done.4, s32[1,1,64,1]{3,2,1,0:T(8,128)S(1)} %copy.11.tile_ref, ...), custom_call_target="tpu_custom_call" | custom-call | flops 60000000 | bytes 5000000 | tf_op jit(solution)/shard_map/coupled_columns/pallas_call | solution.py:460
  72.0 1.0 %copy.13 = f32[1,2,64,16,128]{4,3,2,1,0:T(8,128)} copy(f32[1,2,64,16,128]{4,3,2,1,0:T(8,128)S(1)} %bitcast.3) | data formatting | bytes 2097152
Async XLA Ops:
  0.7 1.6 %copy-start = (bf16[1,1,64,128,128]{4,3,2,1,0:T(8,128)(2,1)S(1)}, bf16[1,1,64,128,128]{4,3,2,1,0:T(8,128)(2,1)}, u32[]{:S(2)}) copy-start(bf16[1,1,64,128,128]{4,3,2,1,0:T(8,128)(2,1)} %param.19) | copy-start | bytes 6291460
  2.3 1.2 %copy-start.1 = (f32[1,2,64,16,128]{4,3,2,1,0:T(8,128)S(1)}, f32[1,2,64,16,128]{4,3,2,1,0:T(8,128)}, u32[]{:S(2)}) copy-start(f32[1,2,64,16,128]{4,3,2,1,0:T(8,128)} %param.10) | copy-start | bytes 3145732
  3.6 0.7 copy-start.2
  4.3 0.7 copy-start.3
  5.0 0.7 copy-start.4
  5.7 0.7 copy-start.5
  6.3 0.7 copy-start.6
  7.0 0.7 copy-start.7
  7.6 0.7 copy-start.8

commit v2 on v1

v2 whole, which is shorter than its diff:
```python
import functools

import jax
import jax.numpy as jnp
from jax import lax
from jax.experimental import pallas as pl
from jax.experimental.pallas import tpu as pltpu
from jax.sharding import PartitionSpec as P

SUBSTEPS = 3
INTERVALS = 2
MESH = pl.DeviceIdType.MESH
HIGHEST = lax.Precision.HIGHEST
TOP = 8
SLAB = 8
LANES = 128
CHUNK = 4


def split_rows(value):
    first = value.astype(jnp.bfloat16)
    rest = value - first.astype(jnp.float32)
    second = rest.astype(jnp.bfloat16)
    third = (rest - second.astype(jnp.float32)).astype(jnp.bfloat16)
    return first, second, third


def pick(onehot, value):
    total = None
    for part in split_rows(value):
        term = jnp.dot(onehot, part, preferred_element_type=jnp.float32)
        total = term if total is None else total + term
    return total


def kernel(
    dims,
    state_ref,
    diff_hbm,
    mix_hbm,
    couple_hbm,
    sea_hbm,
    tile_hbm,
    src_hbm,
    dst_hbm,
    cols_hbm,
    weight_ref,
    out_hbm,
    state_v,
    weight_v,
    out_ref,
    diff_ref,
    mix_ref,
    couple_ref,
    sea_ref,
    tile_ref,
    src_ref,
    dst_ref,
    cols_ref,
    *rest,
):
    n_gx, n_gy, tiles, rows, pairs, tracers, levels, width = dims
    count = INTERVALS * SUBSTEPS
    groups = levels // SLAB
    per_row = LANES // (2 * width)
    pack_rows = -(-groups // per_row) * SLAB
    fields = rest[:count]
    rest = rest[count:]
    slabs = rest[: INTERVALS * (SUBSTEPS - 1)]
    rest = rest[INTERVALS * (SUBSTEPS - 1) :]
    pack_out = rest[: count * tracers]
    pack_in = rest[count * tracers : 2 * count * tracers]
    rest = rest[2 * count * tracers :]
    slab_count = INTERVALS * (SUBSTEPS - 1) + 1
    slab_out = rest[:slab_count]
    slab_in = rest[slab_count : 2 * slab_count]
    rest = rest[2 * slab_count :]
    sends = rest[:INTERVALS]
    recvs = rest[INTERVALS : 2 * INTERVALS]
    rest = rest[2 * INTERVALS :]
    (
        label_out,
        label_in,
        surf,
        contrib,
        gate_diff,
        gate_couple,
        gate_ref,
        mix_v,
        goal,
        onehot_v,
        dense_v,
        load_sem,
        halo_send,
        halo_recv,
        route_send,
        route_recv,
        out_sem,
    ) = rest

    comp = lax.axis_index("comp")
    gx = lax.axis_index("gx")
    gy = lax.axis_index("gy")
    other = 1 - comp
    mine = gx * n_gy + gy
    right = (comp, lax.rem(gx + 1, n_gx), gy)
    left = (comp, lax.rem(gx + n_gx - 1, n_gx), gy)
    across = (comp, gx, lax.rem(gy + 1, n_gy))

    loads = []
    for src, dst in (
        (tile_hbm, tile_ref),
        (dst_hbm, dst_ref),
        (state_ref, state_v),
        (sea_hbm, sea_ref),
        (diff_hbm, diff_ref),
        (couple_hbm, couple_ref),
        (mix_hbm, mix_ref),
        (src_hbm, src_ref),
        (cols_hbm, cols_ref),
        (weight_ref, weight_v),
    ):
        copy = pltpu.make_async_copy(src, dst, load_sem.at[len(loads)])
        copy.start()
        loads.append(copy)

    def peer(step):
        tile = lax.rem(mine + step, tiles)
        return tile, (other, tile // n_gy, lax.rem(tile, n_gy))

    barrier = pltpu.get_barrier_semaphore()
    for device in (right, left, across):
        pl.semaphore_signal(barrier, inc=1, device_id=device, device_id_type=MESH)

    def greet(step, carry):
        pl.semaphore_signal(barrier, inc=1, device_id=peer(step)[1], device_id_type=MESH)
        return carry

    lax.fori_loop(0, tiles, greet, 0)

    loads[0].wait()
    loads[1].wait()
    sub_ids = lax.broadcasted_iota(jnp.int32, (pairs, pairs), 0)
    lane_ids = lax.broadcasted_iota(jnp.int32, (pairs, pairs), 1)
    dest_row = tile_ref[0].astype(jnp.float32)
    dest_wide = jnp.broadcast_to(dest_row, (pairs, pairs))
    dest_col = jnp.sum(jnp.where(sub_ids == lane_ids, dest_wide, 0.0), axis=1, keepdims=True)
    same = dest_col == dest_wide
    rank_row = jnp.sum(jnp.where(same & (sub_ids < lane_ids), 1.0, 0.0), axis=0, keepdims=True)
    rank_col = jnp.sum(jnp.where(same & (lane_ids < sub_ids), 1.0, 0.0), axis=1, keepdims=True)
    place = (dest_row * rows + rank_row).astype(jnp.int32)
    slot_ids = lax.broadcasted_iota(jnp.int32, (tiles * rows, pairs), 0)
    onehot_v[...] = jnp.where(slot_ids == place, 1.0, 0.0).astype(jnp.bfloat16)
    tile_ids = lax.broadcasted_iota(jnp.int32, (tiles, pairs), 0).astype(jnp.float32)
    named = jnp.where(tile_ids == dest_row, (dst_ref[0] + 1).astype(jnp.float32), 0.0)
    slot_lane = lax.broadcasted_iota(jnp.int32, (pairs, LANES), 1).astype(jnp.float32)
    ranked = jnp.where(slot_lane == rank_col, 1.0, 0.0)
    label_out[...] = jnp.dot(
        named.astype(jnp.bfloat16), ranked.astype(jnp.bfloat16), preferred_element_type=jnp.float32
    ).reshape(tiles, 1, LANES)

    surf[...] = jnp.zeros(surf.shape, jnp.float32)

    def lane_of(height):
        return lax.broadcasted_iota(jnp.int32, (height, LANES), 1)

    pairs_lane = lane_of(SLAB) // 2

    def pack_tile(acc, value, j):
        return jnp.where(pairs_lane == j, pltpu.roll(value, 2 * j + 1, 1), acc)

    def unpack_tile(value, j):
        return pltpu.roll(value, LANES - 1 - 2 * j, 1)

    def pack_column(acc, value, x, skip):
        acc = list(acc)
        for g in range(skip, groups):
            part = value[(g - skip) * SLAB : (g - skip + 1) * SLAB]
            acc[g // per_row] = pack_tile(acc[g // per_row], part, (g % per_row) * width + x)
        return tuple(acc)

    def unpack_column(ref, x, skip):
        parts = []
        for g in range(skip, groups):
            low = (g // per_row) * SLAB
            parts.append(unpack_tile(ref[low : low + SLAB, :], (g % per_row) * width + x))
        return parts

    def exchange(number, to_right, to_left, packs):
        copies = []
        for i, (src, dst, device) in enumerate(
            ((packs[0], packs[1], across), (to_right[0], to_right[1], right), (to_left[0], to_left[1], left))
        ):
            copy = pltpu.make_async_remote_copy(
                src_ref=src,
                dst_ref=dst,
                send_sem=halo_send.at[number, i],
                recv_sem=halo_recv.at[number, i],
                device_id=device,
                device_id_type=MESH,
            )
            copy.start()
            copies.append(copy)
        return copies

    def x_sides(buf, f, low, high):
        span = pl.ds(low, high - low)
        to_right = (buf.at[f, width, span, :], buf.at[f, 0, span, :])
        to_left = (buf.at[f, 1, span, :], buf.at[f, width + 1, span, :])
        return to_right, to_left

    started = []
    numbers = iter(range(64))

    def send_halo(buf, f, low, high, out, into):
        copies = exchange(next(numbers), *x_sides(buf, f, low, high), (out, into))
        started.extend(copies)
        return copies

    def stencil(buf, f, x, low, height, turned):
        center = buf[f, x + 1, low : low + height]
        after = buf[f, x + 2, low : low + height]
        before = buf[f, x, low : low + height]
        above = buf[f, x + 1, low - 1 : low - 1 + height]
        below = buf[f, x + 1, low + 1 : low + 1 + height]
        lanes = lane_of(height)
        north = pltpu.roll(jnp.where(lanes == 0, turned, center), LANES - 1, 1)
        south = pltpu.roll(jnp.where(lanes == LANES - 1, turned, center), 1, 1)
        lap_h = (after + before) + (north + south) - 4.0 * center
        lap_v = (below + above) - 2.0 * center
        row = pl.ds(x, 1)
        gd = jnp.broadcast_to(gate_diff[row, :], (height, LANES))
        gv = jnp.broadcast_to(gate_ref[row, :], (height, LANES)) * mix_v[low - TOP : low - TOP + height]
        return center, center + (gd * lap_h + gv * lap_v)

    def with_ends(buf, f, x, value, height):
        buf[f, x + 1, TOP - 1 : TOP] = value[0:1]
        buf[f, x + 1, TOP + height : TOP + height + 1] = value[height - 1 : height]

    pl.semaphore_wait(barrier, tiles + 3)

    def post_all(source, target, number):
        def post(step, carry):
            tile, device = peer(step)
            pltpu.make_async_remote_copy(
                src_ref=source.at[tile],
                dst_ref=target.at[mine],
                send_sem=route_send.at[number],
                recv_sem=route_recv.at[number],
                device_id=device,
                device_id_type=MESH,
            ).start()
            return carry

        lax.fori_loop(0, tiles, post, 0)

    zero = jnp.zeros((SLAB, LANES), jnp.float32)
    empty = (zero,) * (pack_rows // SLAB)

    def store_pack(ref, acc):
        for i, part in enumerate(acc):
            ref[i * SLAB : (i + 1) * SLAB, :] = part

    loads[2].wait()
    pending = []
    for f in range(tracers):

        def load(chunk, acc):
            for i in range(CHUNK):
                x = chunk * CHUNK + i
                value = state_v[pl.ds(f * levels * width + x, levels, stride=width), :]
                fields[0][f, x + 1, TOP : TOP + levels] = value
                with_ends(fields[0], f, x, value, levels)
                surf[x, f : f + 1] = value[0:1]
                acc = pack_column(acc, value, x, 0)
            return acc

        store_pack(pack_out[f], lax.fori_loop(0, width // CHUNK, load, empty))
        pending.append(send_halo(fields[0], f, TOP, TOP + levels, pack_out[f], pack_in[f]))
    post_all(label_out, label_in, INTERVALS)

    for copy in loads[3:]:
        copy.wait()
    sea = sea_ref[0].astype(jnp.float32)
    gate = jnp.where(comp == 1, sea, jnp.ones_like(sea))
    gate_ref[...] = gate
    gate_diff[...] = gate * diff_ref[0]
    gate_couple[...] = gate * couple_ref[0]
    level_a = lax.broadcasted_iota(jnp.int32, (levels, levels), 0)
    level_b = lax.broadcasted_iota(jnp.int32, (levels, levels), 1)
    mix_col = jnp.sum(
        jnp.where(level_a == level_b, jnp.broadcast_to(mix_ref[...], (levels, levels)), 0.0),
        axis=1,
        keepdims=True,
    )
    mix_v[...] = jnp.broadcast_to(mix_col, (levels, LANES))

    def remap(interval):
        lanes = lane_of(SLAB)

        def one(group, carry):
            for i in range(16):
                p = group * 16 + i
                left_side = surf[src_ref[0, 0, p]].astype(jnp.bfloat16)
                got = lax.dot_general(
                    left_side,
                    weight_v[p],
                    (((1,), (1,)), ((), ())),
                    preferred_element_type=jnp.float32,
                )
                got = jnp.where(lanes < cols_ref[0, 0, p], got, 0.0)
                contrib[pl.ds(pl.multiple_of(p * 8, 8), 8), :] = got
            return carry

        lax.fori_loop(0, pairs // 16, one, 0)
        onehot = onehot_v[...]
        for f in range(tracers):
            value = contrib[pl.ds(f, pairs, stride=8), :]
            sends[interval][:, :, f * LANES : (f + 1) * LANES] = pick(onehot, value).reshape(
                tiles, rows, LANES
            )
        post_all(sends[interval], recvs[interval], interval)

    def wait_whole(ref, sem):
        pltpu.make_async_copy(ref, ref, sem).wait()

    out_copies = []

    def write_out(f, low, high):
        span = pl.ds(f * levels * width + low * width, (high - low) * width)
        copy = pltpu.make_async_copy(
            out_ref.at[span, :], out_hbm.at[span, :], out_sem.at[len(out_copies)]
        )
        copy.start()
        out_copies.append(copy)

    inner = max(c for c in range(1, 9) if (width - 2) % c == 0)
    slab_number = 0
    slab_pending = []
    for interval in range(INTERVALS):
        final = interval == INTERVALS - 1
        first = interval * SUBSTEPS
        remap(interval)

        def bulk_step(sub, f):
            buf = fields[first + sub]
            after = None if final and sub == SUBSTEPS - 1 else fields[first + sub + 1]
            pack = pack_in[(first + sub) * tracers + f]
            fresh = sub == 0 and interval > 0
            last = sub == SUBSTEPS - 1
            skip = 1 if last else 0
            low = TOP + skip * SLAB
            height = levels - skip * SLAB
            entry = slab_in[slab_number - 1] if fresh else None

            def column(x, acc):
                parts = unpack_column(pack, x, skip)
                if fresh:
                    parts[0] = unpack_tile(entry[...], f * width + x)
                turned = jnp.concatenate(parts, axis=0)
                _, value = stencil(buf, f, x, low, height, turned)
                if after is None:
                    start = f * levels * width + SLAB * width + x
                    out_ref[pl.ds(start, height, stride=width), :] = value
                    return acc
                after[f, x + 1, low : low + height] = value
                if last:
                    after[f, x + 1, TOP + levels : TOP + levels + 1] = value[height - 1 : height]
                else:
                    with_ends(after, f, x, value, height)
                return pack_column(acc, value, x, skip)

            def chunk(step, acc):
                for i in range(inner):
                    acc = column(1 + step * inner + i, acc)
                return acc

            copies = pending[f]
            copies[0].wait_recv()
            acc = lax.fori_loop(0, (width - 2) // inner, chunk, empty)
            copies[1].wait_recv()
            copies[2].wait_recv()
            acc = column(0, acc)
            acc = column(width - 1, acc)
            if after is None:
                write_out(f, SLAB, levels)
                return
            index = (first + sub + 1) * tracers + f
            store_pack(pack_out[index], acc)
            pending[f] = send_halo(after, f, low, low + height, pack_out[index], pack_in[index])

        def near_step(sub, number, waits):
            for copy in waits:
                copy.wait_recv()
            index = interval * (SUBSTEPS - 1) + sub - 1
            buf = fields[first] if sub == 0 else slabs[index]
            last = sub == SUBSTEPS - 1
            entry = None if sub == 0 and interval == 0 else slab_in[number - 1]
            after = None
            if not last:
                after = slabs[index + 1]
            elif not final:
                after = fields[first + SUBSTEPS]
            acc = zero
            for x in range(width):
                for f in range(tracers):
                    if entry is None:
                        turned = unpack_tile(pack_in[f][0:SLAB, :], x)
                    else:
                        turned = unpack_tile(entry[...], f * width + x)
                    center, value = stencil(buf, f, x, TOP, SLAB, turned)
                    force = jnp.broadcast_to(gate_couple[x : x + 1, :], (SLAB, LANES)) * (
                        jnp.broadcast_to(goal[f, x : x + 1, :], (SLAB, LANES)) - center
                    )
                    sub_row = lax.broadcasted_iota(jnp.int32, (SLAB, LANES), 0)
                    value = value + jnp.where(sub_row == 0, force, 0.0)
                    if after is None:
                        out_ref[pl.ds(f * levels * width + x, SLAB, stride=width), :] = value
                        continue
                    if last:
                        surf[x, f : f + 1] = value[0:1]
                    else:
                        after[f, x + 1, TOP + SLAB : TOP + SLAB + 1] = fields[first + sub + 1][
                            f, x + 1, TOP + SLAB : TOP + SLAB + 1
                        ]
                    after[f, x + 1, TOP : TOP + SLAB] = value
                    after[f, x + 1, TOP - 1 : TOP] = value[0:1]
                    acc = pack_tile(acc, value, f * width + x)
            if after is None:
                return []
            slab_out[number][...] = acc
            both = slice(None)
            return send_halo(after, both, TOP, TOP + SLAB, slab_out[number], slab_in[number])

        for copy in slab_pending:
            copy.wait_recv()
        slab_pending = []
        for sub in range(SUBSTEPS - 1):
            for f in range(tracers):
                bulk_step(sub, f)

        if interval == 0:
            wait_whole(label_in, route_recv.at[INTERVALS])
            heard = label_in[...].reshape(tiles, LANES).astype(jnp.bfloat16)
            slots = tiles * rows
            spread_a = lax.broadcasted_iota(jnp.int32, (LANES, slots), 0)
            spread_b = lax.broadcasted_iota(jnp.int32, (LANES, slots), 1)
            spread = jnp.where(spread_a == spread_b % rows, 1.0, 0.0).astype(jnp.bfloat16)
            table = jnp.dot(heard, spread, preferred_element_type=jnp.float32)
            own_a = lax.broadcasted_iota(jnp.int32, (tiles, slots), 0)
            own_b = lax.broadcasted_iota(jnp.int32, (tiles, slots), 1)
            label_row = jnp.sum(jnp.where(own_a == own_b // rows, table, 0.0), axis=0, keepdims=True)
            block_ids = lax.broadcasted_iota(jnp.int32, (width, slots), 0) + 1
            dense_v[...] = jnp.where(block_ids.astype(jnp.float32) == label_row, 1.0, 0.0).astype(
                jnp.bfloat16
            )
        wait_whole(recvs[interval], route_recv.at[interval])
        dense = dense_v[...]
        for f in range(tracers):
            value = recvs[interval][:, :, f * LANES : (f + 1) * LANES].reshape(tiles * rows, LANES)
            goal[f] = sea * pick(dense, value)

        for sub in range(SUBSTEPS):
            slab_pending = near_step(sub, slab_number, slab_pending)
            if not (sub == SUBSTEPS - 1 and final):
                slab_number += 1
            if sub < tracers:
                bulk_step(SUBSTEPS - 1, sub)

    for f in range(tracers):
        write_out(f, 0, SLAB)
    for copy in started:
        copy.wait_send()
    for interval in range(INTERVALS):
        wait_whole(sends[interval], route_send.at[interval])
    wait_whole(label_out, route_send.at[INTERVALS])
    for copy in out_copies:
        copy.wait()


def body(
    n_gx,
    n_gy,
    state,
    diffusion,
    vertical,
    coupling,
    land_sea,
    route_tile,
    route_src,
    route_dst,
    pair_cols,
    intersection,
):
    _, tracers, levels, width, lanes = state.shape
    assert lanes == LANES and n_gy == 2 and 2 * tracers * width <= LANES
    tiles = n_gx * n_gy
    pairs = route_src.shape[2]
    slots = max(2, 2 * pairs // tiles)
    rows = -(-slots // 8) * 8
    dims = (n_gx, n_gy, tiles, rows, pairs, tracers, levels, width)
    count = INTERVALS * SUBSTEPS
    slab_count = INTERVALS * (SUBSTEPS - 1) + 1
    f32 = jnp.float32
    groups = levels // SLAB
    pack_rows = -(-groups // (LANES // (2 * width))) * SLAB
    halos = count * tracers + slab_count
    scratch = [
        pltpu.VMEM((tracers * levels * width, LANES), f32),
        pltpu.VMEM(intersection.shape[2:], jnp.bfloat16),
        pltpu.VMEM((tracers * levels * width, LANES), f32),
        pltpu.VMEM(diffusion.shape, f32),
        pltpu.VMEM(vertical.shape, f32),
        pltpu.VMEM(coupling.shape, f32),
        pltpu.VMEM(land_sea.shape, jnp.int32),
        pltpu.VMEM(route_src.shape, jnp.int32),
        pltpu.SMEM(route_src.shape, jnp.int32),
        pltpu.VMEM(route_dst.shape, jnp.int32),
        pltpu.SMEM(pair_cols.shape, jnp.int32),
    ]
    scratch += [pltpu.VMEM((tracers, width + 2, TOP + levels + 8, LANES), f32)] * count
    scratch += [pltpu.VMEM((tracers, width + 2, TOP + SLAB + 8, LANES), f32)] * (
        INTERVALS * (SUBSTEPS - 1)
    )
    scratch += [pltpu.VMEM((pack_rows, LANES), f32)] * (2 * count * tracers)
    scratch += [pltpu.VMEM((SLAB, LANES), f32)] * (2 * slab_count)
    scratch += [pltpu.VMEM((tiles, rows, tracers * LANES), f32)] * (2 * INTERVALS)
    scratch += [
        pltpu.VMEM((tiles, 1, LANES), f32),
        pltpu.VMEM((tiles, 1, LANES), f32),
        pltpu.VMEM((width, 8, LANES), f32),
        pltpu.VMEM((pairs * 8, LANES), f32),
        pltpu.VMEM((width, LANES), f32),
        pltpu.VMEM((width, LANES), f32),
        pltpu.VMEM((width, LANES), f32),
        pltpu.VMEM((levels, LANES), f32),
        pltpu.VMEM((tracers, width, LANES), f32),
        pltpu.VMEM((tiles * rows, pairs), jnp.bfloat16),
        pltpu.VMEM((width, tiles * rows), jnp.bfloat16),
        pltpu.SemaphoreType.DMA((10,)),
        pltpu.SemaphoreType.DMA((halos, 3)),
        pltpu.SemaphoreType.DMA((halos, 3)),
        pltpu.SemaphoreType.DMA((INTERVALS + 1,)),
        pltpu.SemaphoreType.DMA((INTERVALS + 1,)),
        pltpu.SemaphoreType.DMA((2 * tracers,)),
    ]
    hbm = pl.BlockSpec(memory_space=pl.ANY)
    out = pl.pallas_call(
        functools.partial(kernel, dims),
        out_shape=jax.ShapeDtypeStruct((tracers * levels * width, LANES), f32),
        in_specs=[hbm] * 10,
        out_specs=hbm,
        scratch_shapes=scratch,
        compiler_params=pltpu.CompilerParams(
            collective_id=0, has_side_effects=True, vmem_limit_bytes=63 * 2**20
        ),
        cost_estimate=pl.CostEstimate(flops=60_000_000, bytes_accessed=5_000_000, transcendentals=0),
        name="coupled_columns",
    )(
        state.reshape(tracers * levels * width, LANES),
        diffusion,
        vertical,
        coupling,
        land_sea,
        route_tile.reshape(route_src.shape),
        route_src,
        route_dst,
        pair_cols,
        intersection.reshape(intersection.shape[2:]),
    )
    return out.reshape(state.shape)


def solution(mesh):
    in_specs = (
        P("comp", None, None, "gx", "gy"),
        P("comp", "gx", "gy"),
        P("comp", None),
        P("comp", "gx", "gy"),
        P("comp", "gx", "gy"),
        P("comp", ("gx", "gy"), None, None),
        P("comp", ("gx", "gy"), None),
        P("comp", ("gx", "gy"), None),
        P("comp", ("gx", "gy"), None),
        P("comp", ("gx", "gy"), None, None, None),
    )
    out_specs = P("comp", None, None, "gx", "gy")
    run = functools.partial(body, mesh.shape["gx"], mesh.shape["gy"])
    return jax.shard_map(run, mesh=mesh, in_specs=in_specs, out_specs=out_specs, check_vma=False)
```

time: 73.3 us -> 45.1 us (0.62)
  Pallas kernels: 63.7 us -> 42.6 us
  local copies, waits for them, and re-layouts: 9.24 us -> 2.26 us
    pallas_call x1, Pallas kernels: 63.7 us -> 42.6 us  [body(): pl.pallas_call(functools.partial(kernel, dims), out_shape=jax.ShapeDtypeS...]
    unnamed x20 -> x1, local copies, waits for them, and re-layouts: 9.24 us -> 2.26 us
where the time goes in v2:
time: 45.1 us; the launch traced here: 44.9 us
  Pallas kernels  42.6 us (94%)
  local copies, waits for them, and re-layouts  2.26 us (5%)
    pallas_call x1, Pallas kernels, body(): pl.pallas_call(functools.partial(kernel, dims), out_shape=jax.ShapeDtypeS...  42.6 us
    unnamed x1, local copies, waits for them, and re-layouts  2.26 us

profile of v2, /device:TPU:0, one launch (start us, length us, event | category | flops | bytes accessed | tf_op | source)
XLA Modules:
  0.0 44.9 jit_solution(5606233071256719748)
XLA Ops:
  0.0 42.6 %coupled_columns.1 = f32[2048,128]{1,0:T(8,128)} custom-call(f32[2048,128]{1,0:T(8,128)} %bitcast.6, f32[1,16,128]{2,1,0:T(8,128)} %diff_hbm.1, f32[1,64]{1,0:T(1,128)} %mix_hbm.1, f32[1,16,128]{2,1,0:T(8,128)} %couple_hbm.1, s32[1,16,128]{2,1,0:T(8,128)} %sea_hbm.1, s32[1,1,64]{2,1,0:T(1,128)} %bitcast.7, s32[1,1,64]{2,1,0:T(1,128)} %src_hbm.1, ...), custom_call_target="tpu_custom_call" | custom-call | flops 60000000 | bytes 5000000 | tf_op jit(solution)/shard_map/coupled_columns/pallas_call | solution.py:548
  42.6 2.3 %copy.12 = f32[1,2,64,16,128]{4,3,2,1,0:T(8,128)} copy(f32[1,2,64,16,128]{4,3,2,1,0:T(8,128)} %bitcast.4) | data formatting | bytes 2097152

commit v3 on v2

--- a/solution.py
+++ b/solution.py
@@ -240,19 +240,20 @@
     pl.semaphore_wait(barrier, tiles + 3)
 
     def post_all(source, target, number):
-        def post(step, carry):
-            tile, device = peer(step)
-            pltpu.make_async_remote_copy(
-                src_ref=source.at[tile],
-                dst_ref=target.at[mine],
-                send_sem=route_send.at[number],
-                recv_sem=route_recv.at[number],
-                device_id=device,
-                device_id_type=MESH,
-            ).start()
+        def post(group, carry):
+            for i in range(4):
+                tile, device = peer(group * 4 + i)
+                pltpu.make_async_remote_copy(
+                    src_ref=source.at[tile],
+                    dst_ref=target.at[mine],
+                    send_sem=route_send.at[number],
+                    recv_sem=route_recv.at[number],
+                    device_id=device,
+                    device_id_type=MESH,
+                ).start()
             return carry
 
-        lax.fori_loop(0, tiles, post, 0)
+        lax.fori_loop(0, tiles // 4, post, 0)
 
     zero = jnp.zeros((SLAB, LANES), jnp.float32)
     empty = (zero,) * (pack_rows // SLAB)
@@ -277,9 +278,52 @@
 
         store_pack(pack_out[f], lax.fori_loop(0, width // CHUNK, load, empty))
         pending.append(send_halo(fields[0], f, TOP, TOP + levels, pack_out[f], pack_in[f]))
+
+    def remap(interval):
+        lanes = lane_of(SLAB)
+
+        def one(group, carry):
+            for i in range(32):
+                p = group * 32 + i
+                left_side = surf[src_ref[0, 0, p]].astype(jnp.bfloat16)
+                got = lax.dot_general(
+                    left_side,
+                    weight_v[p],
+                    (((1,), (1,)), ((), ())),
+                    preferred_element_type=jnp.float32,
+                )
+                got = jnp.where(lanes < cols_ref[0, 0, p], got, 0.0)
+                contrib[pl.ds(pl.multiple_of(p * 8, 8), 8), :] = got
+            return carry
+
+        lax.fori_loop(0, pairs // 32, one, 0)
+        onehot = onehot_v[...]
+        for f in range(tracers):
+            value = contrib[pl.ds(f, pairs, stride=8), :]
+            sends[interval][:, :, f * LANES : (f + 1) * LANES] = pick(onehot, value).reshape(
+                tiles, rows, LANES
+            )
+        post_all(sends[interval], recvs[interval], interval)
+
+    def wait_whole(ref, sem):
+        pltpu.make_async_copy(ref, ref, sem).wait()
+
+    out_copies = []
+
+    def write_out(f, low, high):
+        span = pl.ds(f * levels * width + low * width, (high - low) * width)
+        copy = pltpu.make_async_copy(
+            out_ref.at[span, :], out_hbm.at[span, :], out_sem.at[len(out_copies)]
+        )
+        copy.start()
+        out_copies.append(copy)
+
+    for copy in loads[7:]:
+        copy.wait()
+    remap(0)
     post_all(label_out, label_in, INTERVALS)
 
-    for copy in loads[3:]:
+    for copy in loads[3:7]:
         copy.wait()
     sea = sea_ref[0].astype(jnp.float32)
     gate = jnp.where(comp == 1, sea, jnp.ones_like(sea))
@@ -295,52 +339,14 @@
     )
     mix_v[...] = jnp.broadcast_to(mix_col, (levels, LANES))
 
-    def remap(interval):
-        lanes = lane_of(SLAB)
-
-        def one(group, carry):
-            for i in range(16):
-                p = group * 16 + i
-                left_side = surf[src_ref[0, 0, p]].astype(jnp.bfloat16)
-                got = lax.dot_general(
-                    left_side,
-                    weight_v[p],
-                    (((1,), (1,)), ((), ())),
-                    preferred_element_type=jnp.float32,
-                )
-                got = jnp.where(lanes < cols_ref[0, 0, p], got, 0.0)
-                contrib[pl.ds(pl.multiple_of(p * 8, 8), 8), :] = got
-            return carry
-
-        lax.fori_loop(0, pairs // 16, one, 0)
-        onehot = onehot_v[...]
-        for f in range(tracers):
-            value = contrib[pl.ds(f, pairs, stride=8), :]
-            sends[interval][:, :, f * LANES : (f + 1) * LANES] = pick(onehot, value).reshape(
-                tiles, rows, LANES
-            )
-        post_all(sends[interval], recvs[interval], interval)
-
-    def wait_whole(ref, sem):
-        pltpu.make_async_copy(ref, ref, sem).wait()
-
-    out_copies = []
-
-    def write_out(f, low, high):
-        span = pl.ds(f * levels * width + low * width, (high - low) * width)
-        copy = pltpu.make_async_copy(
-            out_ref.at[span, :], out_hbm.at[span, :], out_sem.at[len(out_copies)]
-        )
-        copy.start()
-        out_copies.append(copy)
-
     inner = max(c for c in range(1, 9) if (width - 2) % c == 0)
     slab_number = 0
     slab_pending = []
     for interval in range(INTERVALS):
         final = interval == INTERVALS - 1
         first = interval * SUBSTEPS
-        remap(interval)
+        if interval > 0:
+            remap(interval)
 
         def bulk_step(sub, f):
             buf = fields[first + sub]
@@ -435,9 +441,8 @@
         for copy in slab_pending:
             copy.wait_recv()
         slab_pending = []
-        for sub in range(SUBSTEPS - 1):
-            for f in range(tracers):
-                bulk_step(sub, f)
+        for f in range(tracers):
+            bulk_step(0, f)
 
         if interval == 0:
             wait_whole(label_in, route_recv.at[INTERVALS])
@@ -464,8 +469,9 @@
             slab_pending = near_step(sub, slab_number, slab_pending)
             if not (sub == SUBSTEPS - 1 and final):
                 slab_number += 1
-            if sub < tracers:
-                bulk_step(SUBSTEPS - 1, sub)
+            if sub < SUBSTEPS - 1:
+                for f in range(tracers):
+                    bulk_step(sub + 1, f)
 
     for f in range(tracers):
         write_out(f, 0, SLAB)
@@ -493,7 +499,7 @@
     intersection,
 ):
     _, tracers, levels, width, lanes = state.shape
-    assert lanes == LANES and n_gy == 2 and 2 * tracers * width <= LANES
+    assert lanes == LANES and n_gy == 2 and 2 * tracers * width <= LANES and n_gx % 2 == 0
     tiles = n_gx * n_gy
     pairs = route_src.shape[2]
     slots = max(2, 2 * pairs // tiles)

time: 45.1 us -> 40.8 us (0.905)
  Pallas kernels: 42.6 us -> 38.4 us
    pallas_call x1, Pallas kernels: 42.6 us -> 38.4 us  [body(): pl.pallas_call(functools.partial(kernel, dims), out_shape=jax.ShapeDtypeS...]
where the time goes in v3:
time: 40.8 us; the launch traced here: 40.6 us
  Pallas kernels  38.4 us (94%)
  local copies, waits for them, and re-layouts  2.26 us (6%)
    pallas_call x1, Pallas kernels, body(): pl.pallas_call(functools.partial(kernel, dims), out_shape=jax.ShapeDtypeS...  38.4 us
    unnamed x1, local copies, waits for them, and re-layouts  2.26 us

profile of v3, /device:TPU:0, one launch (start us, length us, event | category | flops | bytes accessed | tf_op | source)
XLA Modules:
  0.0 40.6 jit_solution(16205821823390810648)
XLA Ops:
  0.0 38.4 %coupled_columns.1 = f32[2048,128]{1,0:T(8,128)} custom-call(f32[2048,128]{1,0:T(8,128)} %bitcast.6, f32[1,16,128]{2,1,0:T(8,128)} %diff_hbm.1, f32[1,64]{1,0:T(1,128)} %mix_hbm.1, f32[1,16,128]{2,1,0:T(8,128)} %couple_hbm.1, s32[1,16,128]{2,1,0:T(8,128)} %sea_hbm.1, s32[1,1,64]{2,1,0:T(1,128)} %bitcast.7, s32[1,1,64]{2,1,0:T(1,128)} %src_hbm.1, ...), custom_call_target="tpu_custom_call" | custom-call | flops 60000000 | bytes 5000000 | tf_op jit(solution)/shard_map/coupled_columns/pallas_call | solution.py:554
  38.4 2.3 %copy.12 = f32[1,2,64,16,128]{4,3,2,1,0:T(8,128)} copy(f32[1,2,64,16,128]{4,3,2,1,0:T(8,128)} %bitcast.4) | data formatting | bytes 2097152

commit v4 on v3

--- a/solution.py
+++ b/solution.py
@@ -68,9 +68,9 @@
     rest = rest[count:]
     slabs = rest[: INTERVALS * (SUBSTEPS - 1)]
     rest = rest[INTERVALS * (SUBSTEPS - 1) :]
-    pack_out = rest[: count * tracers]
-    pack_in = rest[count * tracers : 2 * count * tracers]
-    rest = rest[2 * count * tracers :]
+    pack_out = rest[:count]
+    pack_in = rest[count : 2 * count]
+    rest = rest[2 * count :]
     slab_count = INTERVALS * (SUBSTEPS - 1) + 1
     slab_out = rest[:slab_count]
     slab_in = rest[slab_count : 2 * slab_count]
@@ -179,11 +179,11 @@
             acc[g // per_row] = pack_tile(acc[g // per_row], part, (g % per_row) * width + x)
         return tuple(acc)
 
-    def unpack_column(ref, x, skip):
+    def unpack_column(ref, f, x, skip):
         parts = []
         for g in range(skip, groups):
             low = (g // per_row) * SLAB
-            parts.append(unpack_tile(ref[low : low + SLAB, :], (g % per_row) * width + x))
+            parts.append(unpack_tile(ref[f, low : low + SLAB, :], (g % per_row) * width + x))
         return parts
 
     def exchange(number, to_right, to_left, packs):
@@ -199,7 +199,6 @@
                 device_id=device,
                 device_id_type=MESH,
             )
-            copy.start()
             copies.append(copy)
         return copies
 
@@ -210,10 +209,17 @@
         return to_right, to_left
 
     started = []
-    numbers = iter(range(64))
-
-    def send_halo(buf, f, low, high, out, into):
-        copies = exchange(next(numbers), *x_sides(buf, f, low, high), (out, into))
+
+    def bulk_halo(n, f):
+        low = TOP + (SLAB if n > 0 and n % SUBSTEPS == 0 else 0)
+        sides = x_sides(fields[n], f, low, TOP + levels)
+        return exchange(n * tracers + f, *sides, (pack_out[n].at[f], pack_in[n].at[f]))
+
+    def slab_halo(number, buf):
+        sides = x_sides(buf, slice(None), TOP, TOP + SLAB)
+        copies = exchange(count * tracers + number, *sides, (slab_out[number], slab_in[number]))
+        for copy in copies:
+            copy.start()
         started.extend(copies)
         return copies
 
@@ -237,8 +243,6 @@
         buf[f, x + 1, TOP - 1 : TOP] = value[0:1]
         buf[f, x + 1, TOP + height : TOP + height + 1] = value[height - 1 : height]
 
-    pl.semaphore_wait(barrier, tiles + 3)
-
     def post_all(source, target, number):
         def post(group, carry):
             for i in range(4):
@@ -258,12 +262,11 @@
     zero = jnp.zeros((SLAB, LANES), jnp.float32)
     empty = (zero,) * (pack_rows // SLAB)
 
-    def store_pack(ref, acc):
+    def store_pack(ref, f, acc):
         for i, part in enumerate(acc):
-            ref[i * SLAB : (i + 1) * SLAB, :] = part
+            ref[f, i * SLAB : (i + 1) * SLAB, :] = part
 
     loads[2].wait()
-    pending = []
     for f in range(tracers):
 
         def load(chunk, acc):
@@ -276,8 +279,7 @@
                 acc = pack_column(acc, value, x, 0)
             return acc
 
-        store_pack(pack_out[f], lax.fori_loop(0, width // CHUNK, load, empty))
-        pending.append(send_halo(fields[0], f, TOP, TOP + levels, pack_out[f], pack_in[f]))
+        store_pack(pack_out[0], f, lax.fori_loop(0, width // CHUNK, load, empty))
 
     def remap(interval):
         lanes = lane_of(SLAB)
@@ -303,24 +305,25 @@
             sends[interval][:, :, f * LANES : (f + 1) * LANES] = pick(onehot, value).reshape(
                 tiles, rows, LANES
             )
-        post_all(sends[interval], recvs[interval], interval)
 
     def wait_whole(ref, sem):
         pltpu.make_async_copy(ref, ref, sem).wait()
 
-    out_copies = []
-
-    def write_out(f, low, high):
-        span = pl.ds(f * levels * width + low * width, (high - low) * width)
-        copy = pltpu.make_async_copy(
-            out_ref.at[span, :], out_hbm.at[span, :], out_sem.at[len(out_copies)]
+    def out_copy(f, low, high, number):
+        begin = pl.multiple_of(f * levels * width + low * width, 8)
+        span = pl.ds(begin, (high - low) * width)
+        return pltpu.make_async_copy(
+            out_ref.at[span, :], out_hbm.at[span, :], out_sem.at[number * tracers + f]
         )
-        copy.start()
-        out_copies.append(copy)
 
     for copy in loads[7:]:
         copy.wait()
     remap(0)
+    pl.semaphore_wait(barrier, tiles + 3)
+    for f in range(tracers):
+        for copy in bulk_halo(0, f):
+            copy.start()
+    post_all(sends[0], recvs[0], 0)
     post_all(label_out, label_in, INTERVALS)
 
     for copy in loads[3:7]:
@@ -347,53 +350,58 @@
         first = interval * SUBSTEPS
         if interval > 0:
             remap(interval)
-
-        def bulk_step(sub, f):
-            buf = fields[first + sub]
-            after = None if final and sub == SUBSTEPS - 1 else fields[first + sub + 1]
-            pack = pack_in[(first + sub) * tracers + f]
+            post_all(sends[interval], recvs[interval], interval)
+
+        def bulk_step(sub):
+            n = first + sub
+            buf = fields[n]
+            last = sub == SUBSTEPS - 1
+            after = None if final and last else fields[n + 1]
             fresh = sub == 0 and interval > 0
-            last = sub == SUBSTEPS - 1
             skip = 1 if last else 0
             low = TOP + skip * SLAB
             height = levels - skip * SLAB
             entry = slab_in[slab_number - 1] if fresh else None
 
-            def column(x, acc):
-                parts = unpack_column(pack, x, skip)
-                if fresh:
-                    parts[0] = unpack_tile(entry[...], f * width + x)
-                turned = jnp.concatenate(parts, axis=0)
-                _, value = stencil(buf, f, x, low, height, turned)
+            def per_tracer(f, carry):
+                def column(x, acc):
+                    parts = unpack_column(pack_in[n], f, x, skip)
+                    if fresh:
+                        parts[0] = unpack_tile(entry[...], f * width + x)
+                    turned = jnp.concatenate(parts, axis=0)
+                    _, value = stencil(buf, f, x, low, height, turned)
+                    if after is None:
+                        start = f * levels * width + SLAB * width + x
+                        out_ref[pl.ds(start, height, stride=width), :] = value
+                        return acc
+                    after[f, x + 1, low : low + height] = value
+                    if last:
+                        after[f, x + 1, TOP + levels : TOP + levels + 1] = value[height - 1 : height]
+                    else:
+                        with_ends(after, f, x, value, height)
+                    return pack_column(acc, value, x, skip)
+
+                def chunk(step, acc):
+                    for i in range(inner):
+                        acc = column(1 + step * inner + i, acc)
+                    return acc
+
+                copies = bulk_halo(n, f)
+                copies[0].wait_recv()
+                acc = lax.fori_loop(0, (width - 2) // inner, chunk, empty)
+                copies[1].wait_recv()
+                copies[2].wait_recv()
+                acc = column(0, acc)
+                acc = column(width - 1, acc)
                 if after is None:
-                    start = f * levels * width + SLAB * width + x
-                    out_ref[pl.ds(start, height, stride=width), :] = value
-                    return acc
-                after[f, x + 1, low : low + height] = value
-                if last:
-                    after[f, x + 1, TOP + levels : TOP + levels + 1] = value[height - 1 : height]
-                else:
-                    with_ends(after, f, x, value, height)
-                return pack_column(acc, value, x, skip)
-
-            def chunk(step, acc):
-                for i in range(inner):
-                    acc = column(1 + step * inner + i, acc)
-                return acc
-
-            copies = pending[f]
-            copies[0].wait_recv()
-            acc = lax.fori_loop(0, (width - 2) // inner, chunk, empty)
-            copies[1].wait_recv()
-            copies[2].wait_recv()
-            acc = column(0, acc)
-            acc = column(width - 1, acc)
-            if after is None:
-                write_out(f, SLAB, levels)
-                return
-            index = (first + sub + 1) * tracers + f
-            store_pack(pack_out[index], acc)
-            pending[f] = send_halo(after, f, low, low + height, pack_out[index], pack_in[index])
+                    out_copy(f, SLAB, levels, 0).start()
+                    return carry
+                store_pack(pack_out[n + 1], f, acc)
+                for copy in bulk_halo(n + 1, f):
+                    copy.start()
+                return carry
+
+            lax.fori_loop(0, tracers, per_tracer, 0)
 
         def near_step(sub, number, waits):
             for copy in waits:
@@ -411,7 +419,7 @@
             for x in range(width):
                 for f in range(tracers):
                     if entry is None:
-                        turned = unpack_tile(pack_in[f][0:SLAB, :], x)
+                        turned = unpack_tile(pack_in[0][f, 0:SLAB, :], x)
                     else:
                         turned = unpack_tile(entry[...], f * width + x)
                     center, value = stencil(buf, f, x, TOP, SLAB, turned)
@@ -435,14 +443,12 @@
             if after is None:
                 return []
             slab_out[number][...] = acc
-            both = slice(None)
-            return send_halo(after, both, TOP, TOP + SLAB, slab_out[number], slab_in[number])
+            return slab_halo(number, after)
 
         for copy in slab_pending:
             copy.wait_recv()
         slab_pending = []
-        for f in range(tracers):
-            bulk_step(0, f)
+        bulk_step(0)
 
         if interval == 0:
             wait_whole(label_in, route_recv.at[INTERVALS])
@@ -470,18 +476,22 @@
             if not (sub == SUBSTEPS - 1 and final):
                 slab_number += 1
             if sub < SUBSTEPS - 1:
-                for f in range(tracers):
-                    bulk_step(sub + 1, f)
+                bulk_step(sub + 1)
 
     for f in range(tracers):
-        write_out(f, 0, SLAB)
+        out_copy(f, 0, SLAB, 1).start()
     for copy in started:
         copy.wait_send()
+    for n in range(count):
+        for f in range(tracers):
+            for copy in bulk_halo(n, f):
+                copy.wait_send()
     for interval in range(INTERVALS):
         wait_whole(sends[interval], route_send.at[interval])
     wait_whole(label_out, route_send.at[INTERVALS])
-    for copy in out_copies:
-        copy.wait()
+    for f in range(tracers):
+        out_copy(f, SLAB, levels, 0).wait()
+        out_copy(f, 0, SLAB, 1).wait()
 
 
 def body(
@@ -528,7 +538,7 @@
     scratch += [pltpu.VMEM((tracers, width + 2, TOP + SLAB + 8, LANES), f32)] * (
         INTERVALS * (SUBSTEPS - 1)
     )
-    scratch += [pltpu.VMEM((pack_rows, LANES), f32)] * (2 * count * tracers)
+    scratch += [pltpu.VMEM((tracers, pack_rows, LANES), f32)] * (2 * count)
     scratch += [pltpu.VMEM((SLAB, LANES), f32)] * (2 * slab_count)
     scratch += [pltpu.VMEM((tiles, rows, tracers * LANES), f32)] * (2 * INTERVALS)
     scratch += [

time: 40.8 us -> 39.9 us (0.978)
  Pallas kernels: 38.4 us -> 37.5 us
    pallas_call x1, Pallas kernels: 38.4 us -> 37.5 us  [body(): pl.pallas_call(functools.partial(kernel, dims), out_shape=jax.ShapeDtypeS...]
where the time goes in v4:
time: 39.9 us; the launch traced here: 39.8 us
  Pallas kernels  37.5 us (94%)
  local copies, waits for them, and re-layouts  2.26 us (6%)
    pallas_call x1, Pallas kernels, body(): pl.pallas_call(functools.partial(kernel, dims), out_shape=jax.ShapeDtypeS...  37.5 us
    unnamed x1, local copies, waits for them, and re-layouts  2.26 us

profile of v4, /device:TPU:0, one launch (start us, length us, event | category | flops | bytes accessed | tf_op | source)
XLA Modules:
  0.0 39.8 jit_solution(7629966752875620164)
XLA Ops:
  0.0 37.5 %coupled_columns.1 = f32[2048,128]{1,0:T(8,128)} custom-call(f32[2048,128]{1,0:T(8,128)} %bitcast.6, f32[1,16,128]{2,1,0:T(8,128)} %diff_hbm.1, f32[1,64]{1,0:T(1,128)} %mix_hbm.1, f32[1,16,128]{2,1,0:T(8,128)} %couple_hbm.1, s32[1,16,128]{2,1,0:T(8,128)} %sea_hbm.1, s32[1,1,64]{2,1,0:T(1,128)} %bitcast.7, s32[1,1,64]{2,1,0:T(1,128)} %src_hbm.1, ...), custom_call_target="tpu_custom_call" | custom-call | flops 60000000 | bytes 5000000 | tf_op jit(solution)/shard_map/coupled_columns/pallas_call | solution.py:564
  37.5 2.3 %copy.12 = f32[1,2,64,16,128]{4,3,2,1,0:T(8,128)} copy(f32[1,2,64,16,128]{4,3,2,1,0:T(8,128)} %bitcast.4) | data formatting | bytes 2097152

commit v5 on v4

--- a/solution.py
+++ b/solution.py
@@ -310,10 +310,9 @@
         pltpu.make_async_copy(ref, ref, sem).wait()
 
     def out_copy(f, low, high, number):
-        begin = pl.multiple_of(f * levels * width + low * width, 8)
-        span = pl.ds(begin, (high - low) * width)
+        span = pl.ds(low, high - low)
         return pltpu.make_async_copy(
-            out_ref.at[span, :], out_hbm.at[span, :], out_sem.at[number * tracers + f]
+            out_ref.at[f, :, span, :], out_hbm.at[f, :, span, :], out_sem.at[number * tracers + f]
         )
 
     for copy in loads[7:]:
@@ -371,8 +370,7 @@
                     turned = jnp.concatenate(parts, axis=0)
                     _, value = stencil(buf, f, x, low, height, turned)
                     if after is None:
-                        start = f * levels * width + SLAB * width + x
-                        out_ref[pl.ds(start, height, stride=width), :] = value
+                        out_ref[f, x, SLAB:levels] = value
                         return acc
                     after[f, x + 1, low : low + height] = value
                     if last:
@@ -429,7 +427,7 @@
                     sub_row = lax.broadcasted_iota(jnp.int32, (SLAB, LANES), 0)
                     value = value + jnp.where(sub_row == 0, force, 0.0)
                     if after is None:
-                        out_ref[pl.ds(f * levels * width + x, SLAB, stride=width), :] = value
+                        out_ref[f, x, 0:SLAB] = value
                         continue
                     if last:
                         surf[x, f : f + 1] = value[0:1]
@@ -524,7 +522,7 @@
     scratch = [
         pltpu.VMEM((tracers * levels * width, LANES), f32),
         pltpu.VMEM(intersection.shape[2:], jnp.bfloat16),
-        pltpu.VMEM((tracers * levels * width, LANES), f32),
+        pltpu.VMEM((tracers, width, levels, LANES), f32),
         pltpu.VMEM(diffusion.shape, f32),
         pltpu.VMEM(vertical.shape, f32),
         pltpu.VMEM(coupling.shape, f32),
@@ -563,7 +561,7 @@
     hbm = pl.BlockSpec(memory_space=pl.ANY)
     out = pl.pallas_call(
         functools.partial(kernel, dims),
-        out_shape=jax.ShapeDtypeStruct((tracers * levels * width, LANES), f32),
+        out_shape=jax.ShapeDtypeStruct((tracers, width, levels, LANES), f32),
         in_specs=[hbm] * 10,
         out_specs=hbm,
         scratch_shapes=scratch,
@@ -584,7 +582,7 @@
         pair_cols,
         intersection.reshape(intersection.shape[2:]),
     )
-    return out.reshape(state.shape)
+    return jnp.transpose(out, (0, 2, 1, 3)).reshape(state.shape)
 
 
 def solution(mesh):

time: 39.9 us -> 40.4 us (1.013)
  local copies, waits for them, and re-layouts: 2.26 us -> 2.81 us
    reshape x0 -> x1, local copies, waits for them, and re-layouts: none -> 2.81 us  [body(): return jnp.transpose(out, (0, 2, 1, 3)).reshape(state.shape)]
    unnamed x1 -> x0, local copies, waits for them, and re-layouts: 2.26 us -> none
where the time goes in v5:
time: 40.4 us; the launch traced here: 40.3 us
  Pallas kernels  37.5 us (93%)
  local copies, waits for them, and re-layouts  2.81 us (7%)
    pallas_call x1, Pallas kernels, body(): pl.pallas_call(functools.partial(kernel, dims), out_shape=jax.ShapeDtypeS...  37.5 us
    reshape x1, local copies, waits for them, and re-layouts, body(): return jnp.transpose(out, (0, 2, 1, 3)).reshape(state.shape)  2.81 us

profile of v5, /device:TPU:0, one launch (start us, length us, event | category | flops | bytes accessed | tf_op | source)
XLA Modules:
  0.0 40.3 jit_solution(2668384150463842991)
XLA Ops:
  0.0 37.5 %coupled_columns.1 = f32[2,16,64,128]{3,2,1,0:T(8,128)} custom-call(f32[2048,128]{1,0:T(8,128)} %bitcast.8, f32[1,16,128]{2,1,0:T(8,128)} %diff_hbm.1, f32[1,64]{1,0:T(1,128)} %mix_hbm.1, f32[1,16,128]{2,1,0:T(8,128)} %couple_hbm.1, s32[1,16,128]{2,1,0:T(8,128)} %sea_hbm.1, s32[1,1,64]{2,1,0:T(1,128)} %bitcast.9, s32[1,1,64]{2,1,0:T(1,128)} %src_hbm.1, ...), custom_call_target="tpu_custom_call" | custom-call | flops 60000000 | bytes 5000000 | tf_op jit(solution)/shard_map/coupled_columns/pallas_call | solution.py:562
  37.5 2.8 %copy.11 = f32[1,2,64,16,128]{4,3,2,1,0:T(8,128)} copy(f32[1,2,64,16,128]{4,2,3,1,0:T(8,128)} %bitcast.6) | data formatting | bytes 2097152 | tf_op jit(solution)/shard_map/reshape | solution.py:585
